TPU v7x, 128 devices: a whole 4x4x4 slice. The times are simulated.
128 devices in a mesh: dp: 4 (over z_lo, core), ctx: 32 (over y, x, z_hi).
Axes of the slice: x: 4, y: 4, z: 4 (z_hi: 2, z_lo: 2; z = z_hi * 2 + z_lo), core: 2. Of those that a mesh axis runs over, the one named last changes fastest.
Arguments:
- tokens_in: bfloat16 [4, 4096, 1536], P('dp', 'ctx'), may hold values from -6 to 6
- qkv_weight: bfloat16 [2048, 1536], P(('dp', 'ctx')), may hold values from -0.21875 to 0.21875
- qkv_bias: bfloat16 [2048], P(('dp', 'ctx')), may hold values from -3 to 3
- out_weight: bfloat16 [1536, 1536], P(('dp', 'ctx')), may hold values from -0.625 to 0.625
- norm_gains: bfloat16 [2, 1536], P(None, ('dp', 'ctx')), may hold values from 0.099609375 to 1.8984375
- gate_weight: bfloat16 [8960, 1536], P(('dp', 'ctx')), may hold values from -0.15625 to 0.15625
- up_weight: bfloat16 [8960, 1536], P(('dp', 'ctx')), may hold values from -0.15625 to 0.15625
- down_weight: bfloat16 [8960, 1536], P(('dp', 'ctx')), may hold values from -0.125 to 0.125
- doc_ids: int32 [4, 4096], P('dp'), may hold values from 0 to 2, as said below
- cotangent: bfloat16 [4, 4096, 1536], P('dp', 'ctx'), may hold values from -6 to 6
Outputs:
- layer_out: bfloat16 [4, 4096, 1536], P('dp', 'ctx')
- input_grad: float32 [4, 4096, 1536], P('dp', 'ctx')
- qkv_weight_grad: float32 [2048, 1536], P(('dp', 'ctx'))
- qkv_bias_grad: float32 [2048], P(('dp', 'ctx'))
- out_weight_grad: float32 [1536, 1536], P(('dp', 'ctx'))
- norm_gains_grad: float32 [2, 1536], P(None, ('dp', 'ctx'))
- gate_weight_grad: float32 [8960, 1536], P(('dp', 'ctx'))
- up_weight_grad: float32 [8960, 1536], P(('dp', 'ctx'))
- down_weight_grad: float32 [8960, 1536], P(('dp', 'ctx'))
Inputs may be any that keep to these rules, and one draw needn't show every extreme that they name: `doc_ids`: in every sequence the ids never fall and take exactly the values 0, 1, 2; document 1 begins within the first half of 128 tokens and ends within the last half of 128 tokens; documents 0 and 2 are not empty.
All inputs are finite; a program needn't handle non-finite values.
Results may differ from a plain program's by a relative error of at most 0.033.
Values may be sent and summed in bfloat16 or wider, within the bound.
A program may use at most 512 MiB of HBM per device.

v0:
```python
import jax
import jax.numpy as jnp
from jax import lax
from jax.sharding import PartitionSpec as P

H = 12
KVH = 2
HD = 128
HQ = 1536


norm_eps = 1e-06
rope_base = 1000000.0
doc_kinds = 3


def positions_of(documents):
    index = jnp.arange(documents.shape[0], dtype=jnp.int32)
    kinds = jnp.arange(doc_kinds, dtype=jnp.int32)
    counts = jnp.sum((documents[None, :] == kinds[:, None]).astype(jnp.int32), axis=1)
    starts = jnp.cumsum(counts) - counts
    first = jnp.sum(jnp.where(documents[:, None] == kinds[None, :], starts[None, :], 0), axis=1)
    return index - first


def rope_tables(position):
    half = HD // 2
    inverse = rope_base ** (-(jnp.arange(half, dtype=jnp.float32) * 2.0 / HD))
    angle = position.astype(jnp.float32)[:, None] * inverse[None, :]
    angle = jnp.concatenate([angle, angle], axis=1)
    return (jnp.cos(angle), jnp.sin(angle))


def rotate(vector, cosine, sine):
    half = vector.shape[-1] // 2
    turned = jnp.concatenate([-vector[..., half:], vector[..., :half]], axis=-1)
    return vector * cosine[:, None, :] + turned * sine[:, None, :]


def rotate_back(grad_in, cosine, sine):
    half = grad_in.shape[-1] // 2
    moved = grad_in * sine[:, None, :]
    turned = jnp.concatenate([moved[..., half:], -moved[..., :half]], axis=-1)
    return grad_in * cosine[:, None, :] + turned


def make_forward(rows_in, pieces):
    gate_rows, up_rows, down_rows = pieces
    gate = jnp.einsum("td,fd->tf", rows_in, gate_rows, preferred_element_type=jnp.float32)
    upward = jnp.einsum("td,fd->tf", rows_in, up_rows, preferred_element_type=jnp.float32)
    hidden = (jax.nn.silu(gate) * upward).astype(jnp.bfloat16)
    total = jnp.dot(hidden, down_rows, preferred_element_type=jnp.float32)
    return (total, gate, upward, hidden)


def make_backward(cot_rows, gate_all, upward_all):

    def fold_step(carry, pieces, start):
        gate_rows, up_rows, down_rows = pieces
        hidden_grad = jnp.einsum(
            "td,fd->tf", cot_rows, down_rows, preferred_element_type=jnp.float32
        )
        sigma = jax.nn.sigmoid(gate_all)
        gate_grad = (hidden_grad * upward_all * sigma * (1.0 + gate_all * (1.0 - sigma))).astype(
            jnp.bfloat16
        )
        upward_grad = (hidden_grad * gate_all * sigma).astype(jnp.bfloat16)
        total = jnp.dot(gate_grad, gate_rows, preferred_element_type=jnp.float32)
        total = total + jnp.dot(upward_grad, up_rows, preferred_element_type=jnp.float32)
        return (total, gate_grad, upward_grad)

    return fold_step


def make_ffn_owner(own_gate, own_upward, own_hidden, pieces):
    rows_piece, cot_piece = pieces
    gate_total = jnp.einsum("tf,td->fd", own_gate, rows_piece, preferred_element_type=jnp.float32)
    up_total = jnp.einsum("tf,td->fd", own_upward, rows_piece, preferred_element_type=jnp.float32)
    down_total = jnp.einsum("tf,td->fd", own_hidden, cot_piece, preferred_element_type=jnp.float32)
    return (gate_total, up_total, down_total)


def make_attn_owner(own_qkv, own_attended, pieces):
    normed_piece, branch_piece = pieces
    qkv_total = jnp.einsum("tf,td->fd", own_qkv, normed_piece, preferred_element_type=jnp.float32)
    out_total = jnp.einsum(
        "tf,td->fd", own_attended, branch_piece, preferred_element_type=jnp.float32
    )
    return (qkv_total, out_total)


def local(
    tokens_in,
    qkv_weight,
    qkv_bias,
    out_weight,
    norm_gains,
    gate_weight,
    up_weight,
    down_weight,
    doc_ids,
    cotangent,
):
    block_index = lax.axis_index("ctx")
    inputs = tokens_in[0].astype(jnp.float32)
    count = inputs.shape[0]
    width = inputs.shape[1]
    documents = doc_ids[0]
    length = documents.shape[0]
    key_block = min(512, length)
    num_blocks = length // key_block
    groups = H // KVH
    scale = HD ** (-0.5)
    w_qkv, b_qkv, w_out, gains = (
        lax.all_gather(qkv_weight, ("dp", "ctx"), axis=0, tiled=True),
        lax.all_gather(qkv_bias, ("dp", "ctx"), axis=0, tiled=True),
        lax.all_gather(out_weight, ("dp", "ctx"), axis=0, tiled=True),
        lax.all_gather(norm_gains, ("dp", "ctx"), axis=1, tiled=True),
    )
    gain_one = gains[0].astype(jnp.float32)
    gain_two = gains[1].astype(jnp.float32)
    first_row = block_index * count
    my_rows = first_row + jnp.arange(count, dtype=jnp.int32)
    my_docs = lax.dynamic_slice_in_dim(documents, first_row, count, 0)
    my_pos = lax.dynamic_slice_in_dim(positions_of(documents), first_row, count, 0)
    cosine, sine = rope_tables(my_pos)
    factor_one = lax.rsqrt(jnp.mean(inputs * inputs, axis=-1, keepdims=True) + norm_eps)
    normed_one = (inputs * factor_one * gain_one).astype(jnp.bfloat16)
    qkv = jnp.einsum(
        "td,fd->tf", normed_one, w_qkv, preferred_element_type=jnp.float32
    ) + b_qkv.astype(jnp.float32)
    queries = (
        rotate(qkv[:, :HQ].reshape(count, H, HD), cosine, sine)
        .astype(jnp.bfloat16)
        .reshape(count, KVH, groups, HD)
    )
    keys_mine = rotate(qkv[:, HQ : HQ + KVH * HD].reshape(count, KVH, HD), cosine, sine).astype(
        jnp.bfloat16
    )
    values_mine = qkv[:, HQ + KVH * HD :].reshape(count, KVH, HD).astype(jnp.bfloat16)
    all_keys, all_values = (
        lax.all_gather(keys_mine, "ctx", axis=0, tiled=True),
        lax.all_gather(values_mine, "ctx", axis=0, tiled=True),
    )
    row_limit = first_row + count

    def scores_of(start):
        key_part = lax.dynamic_slice_in_dim(all_keys, start, key_block, 0)
        raw = (
            jnp.einsum("qkgd,skd->kgqs", queries, key_part, preferred_element_type=jnp.float32)
            * scale
        )
        key_rows = start + jnp.arange(key_block, dtype=jnp.int32)
        key_docs = lax.dynamic_slice_in_dim(documents, start, key_block, 0)
        allowed = (key_rows[None, :] <= my_rows[:, None]) & (key_docs[None, :] == my_docs[:, None])
        return (raw, allowed)

    def stats_step(block_id, carry):
        start = block_id * key_block

        def stats_live(state):
            raw, allowed = scores_of(start)
            masked = jnp.where(allowed, raw, -1e30)
            new_top = jnp.maximum(state[0], jnp.max(masked, axis=-1))
            new_total = state[1] * jnp.exp(state[0] - new_top) + jnp.sum(
                jnp.exp(masked - new_top[..., None]), axis=-1
            )
            return (new_top, new_total)

        return lax.cond(start < row_limit, stats_live, lambda state: state, carry)

    stat_shape = (KVH, groups, count)
    top_score, total_exp = lax.fori_loop(
        0,
        num_blocks,
        stats_step,
        (jnp.full(stat_shape, -1e30, jnp.float32), jnp.zeros(stat_shape, jnp.float32)),
    )
    log_total = top_score + jnp.log(total_exp)

    def probs_of(start):
        raw, allowed = scores_of(start)
        return jnp.where(allowed, jnp.exp(raw - log_total[..., None]), 0.0)

    def attend_step(block_id, carry):
        start = block_id * key_block

        def attend_live(state):
            probs = probs_of(start).astype(jnp.bfloat16)
            value_part = lax.dynamic_slice_in_dim(all_values, start, key_block, 0)
            return state + jnp.einsum(
                "kgqs,skd->qkgd", probs, value_part, preferred_element_type=jnp.float32
            )

        return lax.cond(start < row_limit, attend_live, lambda state: state, carry)

    attended = lax.fori_loop(
        0, num_blocks, attend_step, jnp.zeros((count, KVH, groups, HD), jnp.float32)
    )
    attended_low = attended.reshape(count, HQ).astype(jnp.bfloat16)
    middle = inputs + jnp.dot(attended_low, w_out, preferred_element_type=jnp.float32)
    factor_two = lax.rsqrt(jnp.mean(middle * middle, axis=-1, keepdims=True) + norm_eps)
    normed_two = (middle * factor_two * gain_two).astype(jnp.bfloat16)
    units = gate_weight.shape[0] * lax.axis_size("dp") * lax.axis_size("ctx")
    ffn_total, gate_all, upward_all, hidden_all = make_forward(
        normed_two,
        (
            lax.all_gather(gate_weight, ("dp", "ctx"), axis=0, tiled=True),
            lax.all_gather(up_weight, ("dp", "ctx"), axis=0, tiled=True),
            lax.all_gather(down_weight, ("dp", "ctx"), axis=0, tiled=True),
        ),
    )
    layer_out = (middle + ffn_total).astype(jnp.bfloat16)
    cot_low = cotangent[0]
    cot_full = cot_low.astype(jnp.float32)
    backward_init = (
        jnp.zeros((count, width), jnp.float32),
        jnp.zeros((count, units), jnp.bfloat16),
        jnp.zeros((count, units), jnp.bfloat16),
    )
    back_fold = make_backward(cot_low, gate_all, upward_all)
    normed_two_grad, gate_grads, upward_grads = back_fold(
        backward_init,
        (
            lax.all_gather(gate_weight, ("dp", "ctx"), axis=0, tiled=True),
            lax.all_gather(up_weight, ("dp", "ctx"), axis=0, tiled=True),
            lax.all_gather(down_weight, ("dp", "ctx"), axis=0, tiled=True),
        ),
        jnp.int32(0),
    )
    own_gate, own_upward, own_hidden = (
        lax.all_to_all(gate_grads, ("dp", "ctx"), split_axis=1, concat_axis=0, tiled=True),
        lax.all_to_all(upward_grads, ("dp", "ctx"), split_axis=1, concat_axis=0, tiled=True),
        lax.all_to_all(hidden_all, ("dp", "ctx"), split_axis=1, concat_axis=0, tiled=True),
    )
    gate_weight_grad, up_weight_grad, down_weight_grad = make_ffn_owner(
        own_gate,
        own_upward,
        own_hidden,
        (
            lax.all_gather(normed_two, ("dp", "ctx"), axis=0, tiled=True),
            lax.all_gather(cot_low, ("dp", "ctx"), axis=0, tiled=True),
        ),
    )
    scaled_two = gain_two * normed_two_grad
    gain_two_grad = jnp.sum(normed_two_grad * middle * factor_two, axis=0)
    middle_grad = (
        cot_full
        + factor_two * scaled_two
        - middle * factor_two**3 * jnp.mean(scaled_two * middle, axis=-1, keepdims=True)
    )
    branch_grad = middle_grad.astype(jnp.bfloat16)
    attended_grad = (
        jnp.einsum("td,fd->tf", branch_grad, w_out, preferred_element_type=jnp.float32)
        .astype(jnp.bfloat16)
        .reshape(count, KVH, groups, HD)
    )
    delta = jnp.transpose(jnp.sum(attended_grad.astype(jnp.float32) * attended, axis=-1), (1, 2, 0))

    def grad_step(block_id, carry):
        start = block_id * key_block

        def grad_live(state):
            query_grad, key_grads, value_grads = state
            probs = probs_of(start)
            key_part = lax.dynamic_slice_in_dim(all_keys, start, key_block, 0)
            value_part = lax.dynamic_slice_in_dim(all_values, start, key_block, 0)
            prob_grad = jnp.einsum(
                "qkgd,skd->kgqs", attended_grad, value_part, preferred_element_type=jnp.float32
            )
            score_grad = (probs * (prob_grad - delta[..., None])).astype(jnp.bfloat16)
            query_grad = query_grad + jnp.einsum(
                "kgqs,skd->qkgd", score_grad, key_part, preferred_element_type=jnp.float32
            )
            key_term = jnp.einsum(
                "kgqs,qkgd->skd", score_grad, queries, preferred_element_type=jnp.float32
            )
            value_term = jnp.einsum(
                "kgqs,qkgd->skd",
                probs.astype(jnp.bfloat16),
                attended_grad,
                preferred_element_type=jnp.float32,
            )
            key_grads = lax.dynamic_update_slice_in_dim(key_grads, key_term, start, 0)
            value_grads = lax.dynamic_update_slice_in_dim(value_grads, value_term, start, 0)
            return (query_grad, key_grads, value_grads)

        return lax.cond(start < row_limit, grad_live, lambda state: state, carry)

    grad_init = (
        jnp.zeros((count, KVH, groups, HD), jnp.float32),
        jnp.zeros((length, KVH, HD), jnp.float32),
        jnp.zeros((length, KVH, HD), jnp.float32),
    )
    query_grad, key_grads, value_grads = lax.fori_loop(0, num_blocks, grad_step, grad_init)
    key_grad, value_grad = (
        lax.psum_scatter(
            (key_grads * scale).astype(jnp.bfloat16), "ctx", scatter_dimension=0, tiled=True
        ).astype(jnp.float32),
        lax.psum_scatter(
            value_grads.astype(jnp.bfloat16), "ctx", scatter_dimension=0, tiled=True
        ).astype(jnp.float32),
    )
    query_pre = rotate_back((query_grad * scale).reshape(count, H, HD), cosine, sine).reshape(
        count, HQ
    )
    key_pre = rotate_back(key_grad, cosine, sine).reshape(count, KVH * HD)
    qkv_grad = jnp.concatenate(
        [query_pre, key_pre, value_grad.reshape(count, KVH * HD)], axis=1
    ).astype(jnp.bfloat16)
    normed_one_grad = jnp.einsum("tf,fd->td", qkv_grad, w_qkv, preferred_element_type=jnp.float32)
    scaled_one = gain_one * normed_one_grad
    gain_one_grad = jnp.sum(normed_one_grad * inputs * factor_one, axis=0)
    input_grad = (
        middle_grad
        + factor_one * scaled_one
        - inputs * factor_one**3 * jnp.mean(scaled_one * inputs, axis=-1, keepdims=True)
    )
    own_qkv, own_attended = (
        lax.all_to_all(qkv_grad, ("dp", "ctx"), split_axis=1, concat_axis=0, tiled=True),
        lax.all_to_all(attended_low, ("dp", "ctx"), split_axis=1, concat_axis=0, tiled=True),
    )
    qkv_weight_grad, out_weight_grad = make_attn_owner(
        own_qkv,
        own_attended,
        (
            lax.all_gather(normed_one, ("dp", "ctx"), axis=0, tiled=True),
            lax.all_gather(branch_grad, ("dp", "ctx"), axis=0, tiled=True),
        ),
    )
    qkv_bias_grad = jnp.sum(own_qkv.astype(jnp.float32), axis=0)
    gain_terms = jnp.stack([gain_one_grad, gain_two_grad], axis=0)
    norm_gains_grad = lax.psum_scatter(gain_terms, ("dp", "ctx"), scatter_dimension=1, tiled=True)
    return (
        layer_out[None],
        input_grad[None],
        qkv_weight_grad,
        qkv_bias_grad,
        out_weight_grad,
        norm_gains_grad,
        gate_weight_grad,
        up_weight_grad,
        down_weight_grad,
    )


def solution(mesh):
    in_specs = (
        P("dp", "ctx", None),
        P(("dp", "ctx"), None),
        P(("dp", "ctx")),
        P(("dp", "ctx"), None),
        P(None, ("dp", "ctx")),
        P(("dp", "ctx"), None),
        P(("dp", "ctx"), None),
        P(("dp", "ctx"), None),
        P("dp", None),
        P("dp", "ctx", None),
    )
    out_specs = (
        P("dp", "ctx", None),
        P("dp", "ctx", None),
        P(("dp", "ctx"), None),
        P(("dp", "ctx")),
        P(("dp", "ctx"), None),
        P(None, ("dp", "ctx")),
        P(("dp", "ctx"), None),
        P(("dp", "ctx"), None),
        P(("dp", "ctx"), None),
    )
    return jax.shard_map(local, mesh=mesh, in_specs=in_specs, out_specs=out_specs, check_vma=False)
```

profile of v0, /device:TPU:0, one launch (start us, length us, event | category | flops | bytes accessed | tf_op | source)
XLA Modules:
  0.0 3932.0 jit_solution(17224723715801193799)
XLA Ops:
  9.8 316.7 %all-gather.1 = bf16[128,12,2]{1,2,0:T(2,128)(2,1)S(1)} all-gather(bf16[1,12,2]{1,2,0:T(2,128)(2,1)} %bitcast.293), channel_id=1, replica_groups=mesh['dp'=4,'ctx'=32] {'dp','ctx'}, dimensions={0}, use_global_device_ids=true | all-gather | bytes 6192 | tf_op jit(solution)/shard_map/all_gather | solution.py:118
  327.5 71.9 %all-reduce = bf16[2048]{0:T(1024)(128)(2,1)S(1)} all-reduce(bf16[2048]{0:T(1024)(128)(2,1)S(1)} %dynamic-update-slice), channel_id=1, replica_groups=mesh['dp'=4,'ctx'=32] {'dp','ctx'}, use_global_device_ids=true, to_apply=%add | all-reduce | flops 2048 | bytes 8192
  403.8 5.0 convolution_add_fusion.3
  414.7 220.2 %all-gather.32.cloned.1.call-done = bf16[128,12,1536]{2,1,0:T(8,128)(2,1)} async-done(((bf16[1,12,1536]{2,1,0:T(8,128)(2,1)}), bf16[128,12,1536]{2,1,0:T(8,128)(2,1)}) %all-gather.32.cloned.1.call-update) | async-done | bytes 4718608 | tf_op jit(solution)/shard_map/all_gather | solution.py:117
  634.9 8.2 reshape.248
  643.9 72.8 %all-gather.22.cloned.1.call-done = bf16[4096,2,128]{0,2,1:T(8,128)(2,1)} async-done(((bf16[128,2,128]{0,2,1:T(8,128)(2,1)}), bf16[4096,2,128]{0,2,1:T(8,128)(2,1)}) %all-gather.22.cloned.1.call-update) | async-done | bytes 2097168 | tf_op jit(solution)/shard_map/all_gather | solution.py:142
  716.6 3.1 copy.133
  719.8 71.2 %all-gather.20.cloned.1.call-done = bf16[4096,2,128]{2,0,1:T(8,128)(2,1)} async-done(((bf16[128,2,128]{2,0,1:T(8,128)(2,1)}), bf16[4096,2,128]{2,0,1:T(8,128)(2,1)}) %all-gather.20.cloned.1.call-update) | async-done | bytes 2097168 | tf_op jit(solution)/shard_map/all_gather | solution.py:143
  791.0 4.1 copy.132
  795.1 2.7 while.51
  798.7 4.3 while.52
  798.7 4.1 conditional.10
  799.8 3.0 fusion.16
  804.9 3.4 multiply_reduce_fusion.3
  808.5 323.0 %all-gather.34.cloned.1.call-done = bf16[128,70,1536]{2,1,0:T(8,128)(2,1)} async-done(((bf16[1,70,1536]{2,1,0:T(8,128)(2,1)}), bf16[128,70,1536]{2,1,0:T(8,128)(2,1)}) %all-gather.34.cloned.1.call-update) | async-done | bytes 27525136 | tf_op jit(solution)/shard_map/all_gather | solution.py:208
  1131.4 33.5 reshape.250
  1164.9 311.2 %all-gather.36.cloned.1.call-done = bf16[128,70,1536]{2,1,0:T(8,128)(2,1)} async-done(((bf16[1,70,1536]{2,1,0:T(8,128)(2,1)}), bf16[128,70,1536]{2,1,0:T(8,128)(2,1)}) %all-gather.36.cloned.1.call-update) | async-done | bytes 27525136 | tf_op jit(solution)/shard_map/all_gather | solution.py:209
  1476.1 33.4 reshape.252
  1509.5 16.4 fusion.87
  1525.9 16.4 fusion.88
  1542.3 278.6 %all-gather.38.cloned.1.call-done = bf16[128,70,1536]{2,1,0:T(8,128)(2,1)} async-done(((bf16[1,70,1536]{2,1,0:T(8,128)(2,1)}), bf16[128,70,1536]{2,1,0:T(8,128)(2,1)}) %all-gather.38.cloned.1.call-update) | async-done | bytes 27525136 | tf_op jit(solution)/shard_map/all_gather | solution.py:210
  1820.9 33.4 reshape.254
  1854.3 18.9 multiply_convert_fusion
  1873.3 11.6 fusion.89
  1884.9 11.0 multiply_reduce_fusion
  1897.2 4.1 convolution_convert_fusion
  1904.2 9.0 while.53
  1904.2 8.7 conditional.11
  1913.2 5.7 copy.139
  1918.9 3.9 multiply_convert_fusion.3
  1922.8 4.2 copy.168
  1927.1 4.1 copy.140
  1931.2 4.1 copy.170
  1938.9 70.0 %all-to-all-start.1 = ((bf16[128,128,12]{0,2,1:T(8,128)(2,1)}), bf16[128,128,12]{0,2,1:T(8,128)(2,1)S(1)}, u32[]{:S(2)}, u32[]{:S(2)}) async-start(bf16[128,128,12]{0,2,1:T(8,128)(2,1)} %convert_element_type.147), calls=%async_computation.1 | async-start | bytes 1048576 | tf_op jit(solution)/shard_map/all_to_all | solution.py:321
  2008.9 4.2 copy.143
  2013.1 4.1 all_to_all.72
  2017.2 5.2 all-to-all-done.1
  2022.4 5.7 all-to-all-start.2
  2028.1 4.2 copy.145
  2032.4 4.1 all_to_all.76
  2036.5 24.4 all-to-all-done.2
  2060.9 7.0 all-to-all-start.3
  2069.2 4.2 copy.147
  2073.4 4.2 all_to_all.80
  2077.8 22.8 all-to-all-done.3
  2100.5 6.9 all-to-all-start.4
  2109.1 11.8 fusion.58
  2127.7 3.2 copy.176
  2130.8 9.5 all-to-all-done.4
  2142.9 3.2 copy.177
  2146.1 89.2 %reduce-scatter.8.cloned.1.call-done = bf16[128,256]{1,0:T(8,128)(2,1)} async-done(((bf16[4096,256]{1,0:T(8,128)(2,1)}), bf16[128,256]{1,0:T(8,128)(2,1)}) %reduce-scatter.8.cloned.1.call-update) | async-done | bytes 65552
  2236.2 184.4 %reduce-scatter.10.cloned.1.call-done = bf16[128,256]{1,0:T(8,128)(2,1)} async-done(((bf16[4096,256]{1,0:T(8,128)(2,1)}), bf16[128,256]{1,0:T(8,128)(2,1)}) %reduce-scatter.10.cloned.1.call-update) | async-done | bytes 65552
  2421.7 4.7 fusion.67
  2427.2 4.6 all-to-all-start
  2431.9 67.6 %all-reduce.1 = f32[2,1536]{1,0:T(2,128)S(1)} all-reduce(f32[2,1536]{1,0:T(2,128)S(1)} %pad_maximum_fusion.2), channel_id=5, replica_groups=mesh['dp'=4,'ctx'=32] {'dp','ctx'}, use_global_device_ids=true, to_apply=%region_27.28.clone | all-reduce | flops 3072 | bytes 24576
  2503.3 286.7 %all-gather.30.cloned.1.call-done = bf16[1,16384,1536]{2,1,0:T(8,128)(2,1)} async-done(((bf16[1,128,1536]{2,1,0:T(8,128)(2,1)}), bf16[1,16384,1536]{2,1,0:T(8,128)(2,1)}) %all-gather.30.cloned.1.call-update) | async-done | bytes 50331664 | tf_op jit(solution)/shard_map/all_gather | solution.py:242
  2790.1 21.2 fusion.55
  2811.3 351.3 %all-gather.24.cloned.1.call-done = bf16[16384,1536]{1,0:T(8,128)(2,1)} async-done(((bf16[128,1536]{1,0:T(8,128)(2,1)}), bf16[16384,1536]{1,0:T(8,128)(2,1)}) %all-gather.24.cloned.1.call-update) | async-done | bytes 50331664 | tf_op jit(solution)/shard_map/all_gather | solution.py:327
  3162.6 19.4 fusion.70
  3182.0 352.3 %all-gather.28.cloned.1.call-done = bf16[16384,1536]{1,0:T(8,128)(2,1)} async-done(((bf16[128,1536]{1,0:T(8,128)(2,1)}), bf16[16384,1536]{1,0:T(8,128)(2,1)}) %all-gather.28.cloned.1.call-update) | async-done | bytes 50331664 | tf_op jit(solution)/shard_map/all_gather | solution.py:241
  3534.3 20.5 fusion.91
  3554.8 22.1 fusion.92
  3576.9 328.7 %all-gather.26.cloned.1.call-done = bf16[16384,1536]{1,0:T(8,128)(2,1)} async-done(((bf16[128,1536]{1,0:T(8,128)(2,1)}), bf16[16384,1536]{1,0:T(8,128)(2,1)}) %all-gather.26.cloned.1.call-update) | async-done | bytes 50331664 | tf_op jit(solution)/shard_map/all_gather | solution.py:328
  3905.6 19.5 fusion.90
  (212 shorter events, 58.5 us)
Async XLA Ops:
  7.2 396.6 %all-gather.18.cloned.1.call-start = ((), (), s32[]{:S(2)}) async-start(), calls=%async_computation.7 | async-start | bytes 6340608 | tf_op jit(solution)/shard_map/all_gather | solution.py:115
  7.9 627.0 %all-gather.32.cloned.1.call-start = ((), (), s32[]{:S(2)}) async-start(), calls=%async_computation.14 | async-start | bytes 6340608 | tf_op jit(solution)/shard_map/all_gather | solution.py:117
  8.7 708.0 %all-gather.22.cloned.1.call-start = ((), (), s32[]{:S(2)}) async-start(), calls=%async_computation.9 | async-start | bytes 2162688 | tf_op jit(solution)/shard_map/all_gather | solution.py:142
  400.4 3.4 copy-start.17
  400.8 242.7 %copy-start.12 = (f32[128,128]{0,1:T(8,128)}, f32[128,128]{0,1:T(8,128)S(1)}, u32[]{:S(2)}) copy-start(f32[128,128]{0,1:T(8,128)S(1)} %get-tuple-element.1025) | copy-start | bytes 196612
  400.8 242.7 %copy-start.14 = (f32[128,128]{0,1:T(8,128)}, f32[128,128]{0,1:T(8,128)S(1)}, u32[]{:S(2)}) copy-start(f32[128,128]{0,1:T(8,128)S(1)} %get-tuple-element.1026) | copy-start | bytes 196612
  402.6 1.2 copy-start.19
  403.7 5.1 copy-start.7
  409.7 381.3 %all-gather.20.cloned.1.call-start = ((), (), s32[]{:S(2)}) async-start(), calls=%async_computation.8 | async-start | bytes 2162688 | tf_op jit(solution)/shard_map/all_gather | solution.py:143
  410.4 721.0 %all-gather.34.cloned.1.call-start = ((), (), s32[]{:S(2)}) async-start(), calls=%async_computation.15 | async-start | bytes 28532736 | tf_op jit(solution)/shard_map/all_gather | solution.py:208
  411.0 1065.1 %all-gather.36.cloned.1.call-start = ((), (), s32[]{:S(2)}) async-start(), calls=%async_computation.16 | async-start | bytes 28532736 | tf_op jit(solution)/shard_map/all_gather | solution.py:209
  411.6 1409.3 %all-gather.38.cloned.1.call-start = ((), (), s32[]{:S(2)}) async-start(), calls=%async_computation.17 | async-start | bytes 28532736 | tf_op jit(solution)/shard_map/all_gather | solution.py:210
  412.3 1823.0 %reduce-scatter.8.cloned.1.call-start = ((), (), s32[]{:S(2)}) async-start(), calls=%async_computation.18 | async-start | bytes 2162688
  798.7 6.2 copy-start.3
  803.1 1.8 copy-start
  804.9 3.4 copy-start.8
  808.5 717.5 %copy-start.5 = (bf16[128,1536]{1,0:T(8,128)(2,1)}, bf16[128,1536]{1,0:T(8,128)(2,1)S(1)}, u32[]{:S(2)}) copy-start(bf16[128,1536]{1,0:T(8,128)(2,1)S(1)} %multiply_convert_fusion.4) | copy-start | bytes 1179652
  1542.3 312.0 %copy-start.16 = (bf16[1,128,1536]{2,1,0:T(8,128)(2,1)S(1)}, bf16[1,128,1536]{2,1,0:T(8,128)(2,1)}, u32[]{:S(2)}) copy-start(bf16[1,128,1536]{2,1,0:T(8,128)(2,1)} %param.31) | copy-start | bytes 1179652
  1873.3 11.6 copy-start.2
  1897.1 4.4 copy-start.10
  1897.1 4.4 copy-start.6
  1927.1 493.5 %reduce-scatter.10.cloned.1.call-start = ((), (), s32[]{:S(2)}) async-start(), calls=%async_computation.19 | async-start | bytes 2162688
  1931.2 6.8 copy-start.9
  1935.4 854.7 %all-gather.30.cloned.1.call-start = ((), (), s32[]{:S(2)}) async-start(), calls=%async_computation.13 | async-start | bytes 50724864 | tf_op jit(solution)/shard_map/all_gather | solution.py:242
  1936.0 1226.6 %all-gather.24.cloned.1.call-start = ((), (), s32[]{:S(2)}) async-start(), calls=%async_computation.10 | async-start | bytes 50724864 | tf_op jit(solution)/shard_map/all_gather | solution.py:327
  1936.7 1597.6 %all-gather.28.cloned.1.call-start = ((), (), s32[]{:S(2)}) async-start(), calls=%async_computation.12 | async-start | bytes 50724864 | tf_op jit(solution)/shard_map/all_gather | solution.py:241
  1937.3 1968.3 %all-gather.26.cloned.1.call-start = ((), (), s32[]{:S(2)}) async-start(), calls=%async_computation.11 | async-start | bytes 50724864 | tf_op jit(solution)/shard_map/all_gather | solution.py:328
  1938.9 83.5 %all-to-all-start.1 = ((bf16[128,128,12]{0,2,1:T(8,128)(2,1)}), bf16[128,128,12]{0,2,1:T(8,128)(2,1)S(1)}, u32[]{:S(2)}, u32[]{:S(2)}) async-start(bf16[128,128,12]{0,2,1:T(8,128)(2,1)} %convert_element_type.147), calls=%async_computation.1 | async-start | bytes 1048576 | tf_op jit(solution)/shard_map/all_to_all | solution.py:321
  2022.4 38.5 all-to-all-start.2
  2060.9 39.6 %all-to-all-start.3 = ((bf16[128,128,70]{0,2,1:T(8,128)(2,1)}), bf16[128,128,70]{0,2,1:T(8,128)(2,1)}, u32[]{:S(2)}, u32[]{:S(2)}) async-start(bf16[128,128,70]{0,2,1:T(8,128)(2,1)} %all_to_all.76), calls=%async_computation.3 | async-start | bytes 4718592 | tf_op jit(solution)/shard_map/all_to_all | solution.py:233
  2073.4 4.2 copy-start.15
  2077.8 29.8 copy-start.13
  2100.5 39.8 %all-to-all-start.4 = ((bf16[128,128,70]{0,2,1:T(8,128)(2,1)}), bf16[128,128,70]{0,2,1:T(8,128)(2,1)}, u32[]{:S(2)}, u32[]{:S(2)}) async-start(bf16[128,128,70]{0,2,1:T(8,128)(2,1)} %all_to_all.80), calls=%async_computation.4 | async-start | bytes 4718592 | tf_op jit(solution)/shard_map/all_to_all | solution.py:234
  2107.4 1.7 copy-start.1
  2142.9 278.7 %copy-start.4 = (bf16[1,128,1536]{2,1,0:T(8,128)(2,1)S(1)}, bf16[1,128,1536]{2,1,0:T(8,128)(2,1)}, u32[]{:S(2)}) copy-start(bf16[1,128,1536]{2,1,0:T(8,128)(2,1)} %param.22) | copy-start | bytes 1179652
  2142.9 278.7 %copy-start.18 = (f32[1536]{0:T(1024)S(1)}, f32[1536]{0:T(1024)}, u32[]{:S(2)}) copy-start(f32[1536]{0:T(1024)} %copy-done.17) | copy-start | bytes 18436
  2142.9 278.7 %copy-start.20 = (f32[128]{0:T(128)S(1)}, f32[128]{0:T(128)}, u32[]{:S(2)}) copy-start(f32[128]{0:T(128)} %copy-done.19) | copy-start | bytes 1540
  2421.7 78.4 %copy-start.21 = (f32[128]{0:T(128)S(1)}, f32[128]{0:T(128)}, u32[]{:S(2)}) copy-start(f32[128]{0:T(128)} %get-tuple-element.1027) | copy-start | bytes 1540
  2427.2 75.4 %all-to-all-start = ((bf16[128,128,16]{0,2,1:T(8,128)(2,1)}), bf16[128,128,16]{0,2,1:T(8,128)(2,1)S(1)}, u32[]{:S(2)}, u32[]{:S(2)}) async-start(bf16[128,128,16]{0,2,1:T(8,128)(2,1)} %bitcast.273), calls=%async_computation | async-start | bytes 1048576 | tf_op jit(solution)/shard_map/all_to_all | solution.py:320
  3554.8 350.8 %copy-start.11 = (bf16[2,8,128,128]{3,1,2,0:T(8,128)(2,1)S(1)}, bf16[2,8,128,128]{3,1,2,0:T(8,128)(2,1)}, u32[]{:S(2)}) copy-start(bf16[2,8,128,128]{3,1,2,0:T(8,128)(2,1)} %copy.174) | copy-start | bytes 1572868
Sparse Core Ops, SparseCore 0:
  9.7 313.0 all-gather.17
  324.5 310.3 all-gather.31
  638.3 78.3 all-gather.21
  720.2 70.7 all-gather.19
  792.5 338.8 all-gather.33
  1133.0 343.0 all-gather.35
  1477.8 343.0 all-gather.37
  1927.2 308.0 reduce-scatter.7
  2237.8 182.7 reduce-scatter.9
  2422.1 367.8 all-gather.29
  2792.3 370.1 all-gather.23
  3164.7 369.5 all-gather.27
  3536.0 369.5 all-gather.25
where the time goes:
time: 3940 us; the launch traced here: 3930 us
  waiting for transfers between devices  2940 us (75%)
  blocking collectives  456 us (12%)
  matrix products  218 us (6%)
  local copies, waits for them, and re-layouts  190 us (5%)
  starting transfers between devices  94.9 us (2%)
    all_gather x1, waiting for transfers between devices, local(): lax.all_gather(normed_two, ('dp', 'ctx'), axis=0, tiled=True)  352 us
    all_gather x1, waiting for transfers between devices, local(): lax.all_gather(normed_one, ('dp', 'ctx'), axis=0, tiled=True)  351 us
    all_gather x1, waiting for transfers between devices, local(): lax.all_gather(branch_grad, ('dp', 'ctx'), axis=0, tiled=True)  329 us
    all_gather x1, waiting for transfers between devices, local(): lax.all_gather(gate_weight, ('dp', 'ctx'), axis=0, tiled=True)  323 us
    all_gather x1, blocking collectives, local(): lax.all_gather(norm_gains, ('dp', 'ctx'), axis=1, tiled=True)  317 us
    all_gather x1, waiting for transfers between devices, local(): lax.all_gather(up_weight, ('dp', 'ctx'), axis=0, tiled=True)  311 us
    all_gather x1, waiting for transfers between devices, local(): lax.all_gather(cot_low, ('dp', 'ctx'), axis=0, tiled=True)  287 us
    unnamed x15, waiting for transfers between devices  279 us
  transfers between devices with their start and end apart: 18, of which 16 were waited for; matrix products, arithmetic and copies ran while one was open for 7% of the time, Pallas kernels for 0%

commit v1 on v0

v1 whole, which is shorter than its diff:
```python
import functools

import jax
import jax.numpy as jnp
from jax import lax
from jax.experimental import pallas as pl
from jax.experimental.pallas import tpu as pltpu
from jax.sharding import Mesh
from jax.sharding import PartitionSpec as P

H = 12
KVH = 2
HD = 128
HQ = 1536
D = 1536
TOK = 128
ROWS = 80

norm_eps = 1e-06
rope_base = 1000000.0
doc_kinds = 3

AXES = ("zl", "c", "y", "x", "zh")
SIZE = {"zl": 2, "c": 2, "y": 4, "x": 4, "zh": 2}
PARTS_OF = {"z": ("zl", "zh"), "x": ("x",), "y": ("y",), "c": ("c",), "zh": ("zh",)}
REACH = {"z": (1, 2, 3), "x": (1, 2, 3), "y": (1, 2, 3), "c": (1,), "zh": (1,)}
BF = jnp.bfloat16
F32 = jnp.float32
ANY = pl.BlockSpec(memory_space=pl.ANY)
VMEM = pl.BlockSpec(memory_space=pltpu.VMEM)


def here():
    return {a: lax.axis_index(a) for a in AXES}


def peer(me, axis, k):
    to = dict(me)
    if axis == "z":
        z = lax.rem(me["zh"] * 2 + me["zl"] + k, 4)
        to["zl"], to["zh"] = lax.rem(z, 2), lax.div(z, 2)
    else:
        to[axis] = lax.rem(me[axis] + k, SIZE[axis])
    return to


def device_id(at):
    return tuple(at[a] for a in AXES)


def place(dims, at, whole, tail=()):
    return tuple(slice(None) if d in whole else at[d] for d in dims) + tuple(tail)


class Links:
    def __init__(self, me, send, recv):
        self.me, self.send, self.recv, self.used = me, send, recv, 0

    def copy(self, src, dst, axis, k):
        i = self.used
        self.used += 1
        c = pltpu.make_async_remote_copy(
            src_ref=src,
            dst_ref=dst,
            send_sem=self.send.at[i],
            recv_sem=self.recv.at[i],
            device_id=device_id(peer(self.me, axis, k)),
            device_id_type=pl.DeviceIdType.MESH,
        )
        c.start()
        return c


def greet(me, axes):
    barrier = pltpu.get_barrier_semaphore()
    count = 0
    for axis in axes:
        for k in REACH[axis]:
            pl.semaphore_signal(
                barrier,
                inc=1,
                device_id=device_id(peer(me, axis, k)),
                device_id_type=pl.DeviceIdType.MESH,
            )
            count += 1
    pl.semaphore_wait(barrier, count)


def gather_stream(links, block, buf, dims, tail, order):
    me = links.me
    whole = ()
    for n, axis in enumerate(order):
        mine = place(dims, me, whole, tail)
        src = block if n == 0 else buf.at[mine]
        copies = [links.copy(src, buf.at[mine], axis, k) for k in REACH[axis]]
        yield
        for c in copies:
            c.wait()
        whole = whole + PARTS_OF[axis]


def run_streams(streams):
    live = list(streams)
    while live:
        live = [s for s in live if next(s, live) is not live]


def count_gather(orders):
    return sum(len(REACH[a]) for order in orders for a in order)


THIRDS = tuple((slice(None), slice(512 * i, 512 * (i + 1))) for i in range(3))
ORDERS = (("x", "y", "z"), ("y", "z", "x"), ("z", "x", "y"))
HALVES = tuple((slice(None), slice(768 * i, 768 * (i + 1))) for i in range(2))
FFN_ORDERS = (("y", "z"), ("z", "y"))
FFN_DIMS = ("zl", "y", "zh")
ROW_DIMS = ("x", "c")
KV_DIMS = ("y", "x", "zh")


def weights_kernel(*refs):
    qkv, out, gate, up, down, cot = refs[:6]
    qkv_all, out_all, gate_all, up_all, down_all, cot_all = refs[6:12]
    send, recv, local = refs[12:]
    me = here()
    links = Links(me, send, recv)
    own = []
    pairs = [
        (qkv, qkv_all, AXES),
        (out, out_all, AXES),
        (gate, gate_all, FFN_DIMS),
        (up, up_all, FFN_DIMS),
        (down, down_all, FFN_DIMS),
        (cot, cot_all, ROW_DIMS),
    ]
    for i, (a, b, dims) in enumerate(pairs):
        own.append(pltpu.make_async_copy(a, b.at[place(dims, me, ())], local.at[i]))
        own[-1].start()
    greet(me, ("x", "y", "z", "c"))
    for c in own:
        c.wait()
    streams = []
    for block, buf in ((qkv, qkv_all), (out, out_all)):
        for order, tail in zip(ORDERS, THIRDS, strict=True):
            streams.append(
                gather_stream(links, block.at[tail], buf, AXES, tail, order + ("c",))
            )
    streams.append(gather_stream(links, cot, cot_all, ROW_DIMS, (), ("x", "c")))
    for block, buf in ((gate, gate_all), (up, up_all), (down, down_all)):
        for order, tail in zip(FFN_ORDERS, HALVES, strict=True):
            streams.append(gather_stream(links, block.at[tail], buf, FFN_DIMS, tail, order))
    run_streams(streams)


def gather_weights(qkv, out, gate, up, down, cot):
    ffn = jax.ShapeDtypeStruct((2, 4, 2, ROWS, D), BF)
    every = jax.ShapeDtypeStruct((2, 2, 4, 4, 2, 16, D), BF)
    rows = jax.ShapeDtypeStruct((4, 2, TOK, D), BF)
    copies = 2 * count_gather([o + ("c",) for o in ORDERS]) + count_gather([("x", "c")])
    copies += 3 * count_gather(FFN_ORDERS)
    return pl.pallas_call(
        weights_kernel,
        out_shape=(every, every, ffn, ffn, ffn, rows),
        in_specs=[ANY] * 6,
        out_specs=(ANY,) * 6,
        scratch_shapes=[
            pltpu.SemaphoreType.DMA((copies,)),
            pltpu.SemaphoreType.DMA((copies,)),
            pltpu.SemaphoreType.DMA((6,)),
        ],
        compiler_params=pltpu.CompilerParams(collective_id=1, has_side_effects=True),
    )(qkv, out, gate, up, down, cot)


def keys_kernel(block, buf, send, recv, local):
    me = here()
    links = Links(me, send, recv)
    own = pltpu.make_async_copy(block, buf.at[place(KV_DIMS, me, ())], local)
    own.start()
    greet(me, ("zh", "x", "y"))
    own.wait()
    streams = []
    for half, order in enumerate((("zh", "x", "y"), ("zh", "y", "x"))):
        tail = (slice(None), slice(256 * half, 256 * (half + 1)))
        streams.append(gather_stream(links, block.at[tail], buf, KV_DIMS, tail, order))
    run_streams(streams)


def gather_keys(block):
    copies = 2 * count_gather([("zh", "x", "y")])
    return pl.pallas_call(
        keys_kernel,
        out_shape=jax.ShapeDtypeStruct((4, 4, 2, TOK, 512), BF),
        in_specs=[ANY],
        out_specs=ANY,
        scratch_shapes=[
            pltpu.SemaphoreType.DMA((copies,)),
            pltpu.SemaphoreType.DMA((copies,)),
            pltpu.SemaphoreType.DMA,
        ],
        compiler_params=pltpu.CompilerParams(collective_id=2, has_side_effects=True),
    )(block)


def rows_kernel(block, buf, send, recv, local):
    me = here()
    links = Links(me, send, recv)
    own = pltpu.make_async_copy(block, buf.at[place(ROW_DIMS, me, ())], local)
    own.start()
    greet(me, ("x", "c"))
    own.wait()
    run_streams([gather_stream(links, block, buf, ROW_DIMS, (), ("x", "c"))])


def gather_rows(block):
    copies = count_gather([("x", "c")])
    return pl.pallas_call(
        rows_kernel,
        out_shape=jax.ShapeDtypeStruct((4, 2, TOK, D), BF),
        in_specs=[ANY],
        out_specs=ANY,
        scratch_shapes=[
            pltpu.SemaphoreType.DMA((copies,)),
            pltpu.SemaphoreType.DMA((copies,)),
            pltpu.SemaphoreType.DMA,
        ],
        compiler_params=pltpu.CompilerParams(collective_id=3, has_side_effects=True),
    )(block)


def lead_of(dims):
    return tuple(SIZE[d] for d in dims)


def rest_of(dims, axis):
    return tuple(d for d in dims if d not in PARTS_OF[axis])


def scatter_scratch(dims, order, rows, cols):
    shapes = []
    for axis in order:
        dims = rest_of(dims, axis)
        shapes.append(pltpu.VMEM((len(REACH[axis]),) + lead_of(dims) + (rows, cols), BF))
        shapes.append(pltpu.VMEM(lead_of(dims) + (rows, cols), BF))
    return shapes


def sum_blocks(own, arrived, out, lead, rows, step):
    count = 1
    for n in lead:
        count *= n
    per = rows // step
    parts = arrived.shape[0]

    def body(i, carry):
        block, row = lax.div(i, per), lax.rem(i, per)
        index = []
        for n in reversed(lead):
            index.append(lax.rem(block, n))
            block = lax.div(block, n)
        at = tuple(reversed(index)) + (pl.ds(pl.multiple_of(row * step, step), step),)
        total = own[at].astype(F32)
        for p in range(parts):
            total = total + arrived[(p,) + at].astype(F32)
        out[at] = total.astype(out.dtype)
        return carry

    lax.fori_loop(0, count * per, body, 0)


def scatter_stream(links, local, source, dims, tail, order, scratch, out, rows, step):
    me = links.me
    now = None
    for n, axis in enumerate(order):
        arrived, own = scratch[2 * n], scratch[2 * n + 1]
        gone = PARTS_OF[axis]
        keep = tuple(d for d in dims if d not in gone)
        end = tail if n == 0 else ()
        base = source if n == 0 else now
        copies = []
        for k in REACH[axis]:
            to = peer(me, axis, k)
            src = base.at[place(dims, to, keep, end)]
            copies.append(links.copy(src, arrived.at[k - 1], axis, k))
        held = base.at[place(dims, me, keep, end)]
        if n == 0:
            mine = pltpu.make_async_copy(held, own, local)
            mine.start()
        yield
        if n == 0:
            mine.wait()
            held = own
        for c in copies:
            c.wait()
        target = out if n == len(order) - 1 else own
        sum_blocks(held, arrived, target, lead_of(keep), rows, step)
        now, dims = own, keep


def rows_scatter_kernel(first, second, out_a, out_b, send, recv, local, *scratch):
    me = here()
    links = Links(me, send, recv)
    greet(me, ("x", "c"))
    half = len(scratch) // 2
    run_streams(
        [
            scatter_stream(
                links, local.at[0], first, ROW_DIMS, (), ("c", "x"), scratch[:half], out_a, TOK, 16
            ),
            scatter_stream(
                links, local.at[1], second, ROW_DIMS, (), ("c", "x"), scratch[half:], out_b, TOK, 16
            ),
        ]
    )


def scatter_rows(first, second):
    copies = 2 * count_gather([("c", "x")])
    one = jax.ShapeDtypeStruct((TOK, D), F32)
    return pl.pallas_call(
        rows_scatter_kernel,
        out_shape=(one, one),
        in_specs=[ANY] * 2,
        out_specs=(VMEM,) * 2,
        scratch_shapes=[
            pltpu.SemaphoreType.DMA((copies,)),
            pltpu.SemaphoreType.DMA((copies,)),
            pltpu.SemaphoreType.DMA((2,)),
        ]
        + 2 * scatter_scratch(ROW_DIMS, ("c", "x"), TOK, D),
        compiler_params=pltpu.CompilerParams(
            collective_id=4, has_side_effects=True, vmem_limit_bytes=48 * 2**20
        ),
    )(first, second)


KV_ORDERS = (("y", "x", "zh"), ("x", "y", "zh"))


def keys_scatter_kernel(source, out, send, recv, local, *scratch):
    me = here()
    links = Links(me, send, recv)
    greet(me, ("zh", "x", "y"))
    streams = []
    for half, order in enumerate(KV_ORDERS):
        tail = (slice(None), slice(256 * half, 256 * (half + 1)))
        part = scratch[6 * half : 6 * half + 6]
        streams.append(
            scatter_stream(
                links, local.at[half], source, KV_DIMS, tail, order, part, out.at[half], TOK, 32
            )
        )
    run_streams(streams)


def scatter_keys(source):
    copies = count_gather(KV_ORDERS)
    return pl.pallas_call(
        keys_scatter_kernel,
        out_shape=jax.ShapeDtypeStruct((2, TOK, 256), F32),
        in_specs=[ANY],
        out_specs=VMEM,
        scratch_shapes=[
            pltpu.SemaphoreType.DMA((copies,)),
            pltpu.SemaphoreType.DMA((copies,)),
            pltpu.SemaphoreType.DMA((2,)),
        ]
        + [s for order in KV_ORDERS for s in scatter_scratch(KV_DIMS, order, TOK, 256)],
        compiler_params=pltpu.CompilerParams(
            collective_id=5, has_side_effects=True, vmem_limit_bytes=48 * 2**20
        ),
    )(source)


ALL_ORDERS = tuple(("c",) + o for o in ORDERS)


def weight_grads_kernel(*refs):
    sources, outs = refs[:5], refs[5:10]
    send, recv, local = refs[10:13]
    scratch = list(refs[13:])
    me = here()
    links = Links(me, send, recv)
    greet(me, ("x", "y", "z", "c"))
    streams = []
    used = 0
    for source, out in zip(sources[:2], outs[:2], strict=True):
        for order, tail in zip(ALL_ORDERS, THIRDS, strict=True):
            part, scratch = scratch[:8], scratch[8:]
            streams.append(
                scatter_stream(
                    links, local.at[used], source, AXES, tail, order, part, out.at[tail], 16, 16
                )
            )
            used += 1
    for source, out in zip(sources[2:], outs[2:], strict=True):
        for order, tail in zip(FFN_ORDERS, HALVES, strict=True):
            part, scratch = scratch[:4], scratch[4:]
            streams.append(
                scatter_stream(
                    links, local.at[used], source, FFN_DIMS, tail, order, part, out.at[tail], ROWS, 16
                )
            )
            used += 1
    run_streams(streams)


def scatter_weight_grads(qkv, out, gate, up, down):
    copies = 2 * count_gather(ALL_ORDERS) + 3 * count_gather(FFN_ORDERS)
    scratch = []
    for _ in range(2):
        for order in ALL_ORDERS:
            scratch += scatter_scratch(AXES, order, 16, 512)
    for _ in range(3):
        for order in FFN_ORDERS:
            scratch += scatter_scratch(FFN_DIMS, order, ROWS, 768)
    attn = jax.ShapeDtypeStruct((16, D), F32)
    ffn = jax.ShapeDtypeStruct((ROWS, D), F32)
    return pl.pallas_call(
        weight_grads_kernel,
        out_shape=(attn, attn, ffn, ffn, ffn),
        in_specs=[ANY] * 5,
        out_specs=(VMEM,) * 5,
        scratch_shapes=[
            pltpu.SemaphoreType.DMA((copies,)),
            pltpu.SemaphoreType.DMA((copies,)),
            pltpu.SemaphoreType.DMA((12,)),
        ]
        + scratch,
        compiler_params=pltpu.CompilerParams(
            collective_id=6, has_side_effects=True, vmem_limit_bytes=60 * 2**20
        ),
    )(qkv, out, gate, up, down)


def positions_of(documents):
    index = jnp.arange(documents.shape[0], dtype=jnp.int32)
    kinds = jnp.arange(doc_kinds, dtype=jnp.int32)
    counts = jnp.sum((documents[None, :] == kinds[:, None]).astype(jnp.int32), axis=1)
    starts = jnp.cumsum(counts) - counts
    first = jnp.sum(jnp.where(documents[:, None] == kinds[None, :], starts[None, :], 0), axis=1)
    return index - first


def rope_tables(position):
    half = HD // 2
    inverse = rope_base ** (-(jnp.arange(half, dtype=jnp.float32) * 2.0 / HD))
    angle = position.astype(jnp.float32)[:, None] * inverse[None, :]
    angle = jnp.concatenate([angle, angle], axis=1)
    return (jnp.cos(angle), jnp.sin(angle))


def rotate(vector, cosine, sine):
    half = vector.shape[-1] // 2
    turned = jnp.concatenate([-vector[..., half:], vector[..., :half]], axis=-1)
    return vector * cosine[:, None, :] + turned * sine[:, None, :]


def rotate_back(grad_in, cosine, sine):
    half = grad_in.shape[-1] // 2
    moved = grad_in * sine[:, None, :]
    turned = jnp.concatenate([moved[..., half:], -moved[..., :half]], axis=-1)
    return grad_in * cosine[:, None, :] + turned


def dot(a, b, dims):
    return lax.dot_general(a, b, ((dims[:1], dims[1:]), ((), ())), preferred_element_type=F32)


def local(
    tokens_in,
    qkv_weight,
    qkv_bias,
    out_weight,
    norm_gains,
    gate_weight,
    up_weight,
    down_weight,
    doc_ids,
    cotangent,
):
    block_index = lax.axis_index("y") * 8 + lax.axis_index("x") * 2 + lax.axis_index("zh")
    inputs = tokens_in[0].astype(F32)
    count = TOK
    documents = doc_ids[0]
    length = documents.shape[0]
    key_block = min(512, length)
    num_blocks = length // key_block
    groups = H // KVH
    scale = HD ** (-0.5)
    cot_low = cotangent[0]

    small = jnp.concatenate([qkv_bias, norm_gains.reshape(-1), jnp.zeros((D - 40,), BF)])[None]
    out_block = jnp.concatenate([out_weight, small, jnp.zeros((3, D), BF)], axis=0)
    pad = ((0, ROWS - gate_weight.shape[0]), (0, 0))
    qkv_all, out_all, gate_all_w, up_all_w, down_all_w, cot_rows = gather_weights(
        qkv_weight,
        out_block,
        jnp.pad(gate_weight, pad),
        jnp.pad(up_weight, pad),
        jnp.pad(down_weight, pad),
        cot_low,
    )
    w_qkv = qkv_all.reshape(2048, D)
    out_all = out_all.reshape(128, 16, D)
    w_out = out_all[:, :12].reshape(HQ, D)
    b_qkv = out_all[:, 12, :16].reshape(2048)
    gain_one = out_all[:, 12, 16:28].reshape(D).astype(F32)
    gain_two = out_all[:, 12, 28:40].reshape(D).astype(F32)
    w_gate = gate_all_w.reshape(-1, D)
    w_up = up_all_w.reshape(-1, D)
    w_down = down_all_w.reshape(-1, D)
    cot_rows = cot_rows.reshape(-1, D)

    first_row = block_index * count
    my_rows = first_row + jnp.arange(count, dtype=jnp.int32)
    my_docs = lax.dynamic_slice_in_dim(documents, first_row, count, 0)
    my_pos = lax.dynamic_slice_in_dim(positions_of(documents), first_row, count, 0)
    cosine, sine = rope_tables(my_pos)
    factor_one = lax.rsqrt(jnp.mean(inputs * inputs, axis=-1, keepdims=True) + norm_eps)
    normed_one = (inputs * factor_one * gain_one).astype(BF)
    qkv = dot(normed_one, w_qkv, (1, 1)) + b_qkv.astype(F32)
    queries = (
        rotate(qkv[:, :HQ].reshape(count, H, HD), cosine, sine)
        .astype(BF)
        .reshape(count, KVH, groups, HD)
    )
    keys_mine = rotate(qkv[:, HQ : HQ + KVH * HD].reshape(count, KVH, HD), cosine, sine).astype(BF)
    keys_values = gather_keys(
        jnp.concatenate(
            [keys_mine.reshape(count, KVH * HD), qkv[:, HQ + KVH * HD :].astype(BF)], axis=1
        )
    ).reshape(length, 2, KVH, HD)
    all_keys, all_values = keys_values[:, 0], keys_values[:, 1]
    row_limit = first_row + count

    def scores_of(start):
        key_part = lax.dynamic_slice_in_dim(all_keys, start, key_block, 0)
        raw = jnp.einsum("qkgd,skd->kgqs", queries, key_part, preferred_element_type=F32) * scale
        key_rows = start + jnp.arange(key_block, dtype=jnp.int32)
        key_docs = lax.dynamic_slice_in_dim(documents, start, key_block, 0)
        allowed = (key_rows[None, :] <= my_rows[:, None]) & (key_docs[None, :] == my_docs[:, None])
        return (raw, allowed)

    def stats_step(block_id, carry):
        start = block_id * key_block

        def stats_live(state):
            raw, allowed = scores_of(start)
            masked = jnp.where(allowed, raw, -1e30)
            new_top = jnp.maximum(state[0], jnp.max(masked, axis=-1))
            new_total = state[1] * jnp.exp(state[0] - new_top) + jnp.sum(
                jnp.exp(masked - new_top[..., None]), axis=-1
            )
            return (new_top, new_total)

        return lax.cond(start < row_limit, stats_live, lambda state: state, carry)

    stat_shape = (KVH, groups, count)
    top_score, total_exp = lax.fori_loop(
        0,
        num_blocks,
        stats_step,
        (jnp.full(stat_shape, -1e30, F32), jnp.zeros(stat_shape, F32)),
    )
    log_total = top_score + jnp.log(total_exp)

    def probs_of(start):
        raw, allowed = scores_of(start)
        return jnp.where(allowed, jnp.exp(raw - log_total[..., None]), 0.0)

    def attend_step(block_id, carry):
        start = block_id * key_block

        def attend_live(state):
            probs = probs_of(start).astype(BF)
            value_part = lax.dynamic_slice_in_dim(all_values, start, key_block, 0)
            return state + jnp.einsum(
                "kgqs,skd->qkgd", probs, value_part, preferred_element_type=F32
            )

        return lax.cond(start < row_limit, attend_live, lambda state: state, carry)

    attended = lax.fori_loop(
        0, num_blocks, attend_step, jnp.zeros((count, KVH, groups, HD), F32)
    )
    attended_low = attended.reshape(count, HQ).astype(BF)
    middle = inputs + dot(attended_low, w_out, (1, 0))
    factor_two = lax.rsqrt(jnp.mean(middle * middle, axis=-1, keepdims=True) + norm_eps)
    normed_two = (middle * factor_two * gain_two).astype(BF)

    rows_two = gather_rows(normed_two).reshape(-1, D)
    gate = dot(rows_two, w_gate, (1, 1))
    upward = dot(rows_two, w_up, (1, 1))
    hidden_grad = dot(cot_rows, w_down, (1, 1))
    sigma = jax.nn.sigmoid(gate)
    hidden = (gate * sigma * upward).astype(BF)
    gate_grad = (hidden_grad * upward * sigma * (1.0 + gate * (1.0 - sigma))).astype(BF)
    upward_grad = (hidden_grad * gate * sigma).astype(BF)
    ffn_part = dot(hidden, w_down, (1, 0)).astype(BF)
    grad_part = (dot(gate_grad, w_gate, (1, 0)) + dot(upward_grad, w_up, (1, 0))).astype(BF)
    ffn_total, normed_two_grad = scatter_rows(
        ffn_part.reshape(4, 2, TOK, D), grad_part.reshape(4, 2, TOK, D)
    )
    layer_out = (middle + ffn_total).astype(BF)

    cot_full = cot_low.astype(F32)
    scaled_two = gain_two * normed_two_grad
    gain_two_grad = jnp.sum(normed_two_grad * middle * factor_two, axis=0)
    middle_grad = (
        cot_full
        + factor_two * scaled_two
        - middle * factor_two**3 * jnp.mean(scaled_two * middle, axis=-1, keepdims=True)
    )
    branch_grad = middle_grad.astype(BF)
    attended_grad = dot(branch_grad, w_out, (1, 1)).astype(BF).reshape(count, KVH, groups, HD)
    delta = jnp.transpose(jnp.sum(attended_grad.astype(F32) * attended, axis=-1), (1, 2, 0))

    def grad_step(block_id, carry):
        start = block_id * key_block

        def grad_live(state):
            query_grad, key_grads, value_grads = state
            probs = probs_of(start)
            key_part = lax.dynamic_slice_in_dim(all_keys, start, key_block, 0)
            value_part = lax.dynamic_slice_in_dim(all_values, start, key_block, 0)
            prob_grad = jnp.einsum(
                "qkgd,skd->kgqs", attended_grad, value_part, preferred_element_type=F32
            )
            score_grad = (probs * (prob_grad - delta[..., None])).astype(BF)
            query_grad = query_grad + jnp.einsum(
                "kgqs,skd->qkgd", score_grad, key_part, preferred_element_type=F32
            )
            key_term = jnp.einsum(
                "kgqs,qkgd->skd", score_grad, queries, preferred_element_type=F32
            )
            value_term = jnp.einsum(
                "kgqs,qkgd->skd", probs.astype(BF), attended_grad, preferred_element_type=F32
            )
            key_grads = lax.dynamic_update_slice_in_dim(key_grads, key_term, start, 0)
            value_grads = lax.dynamic_update_slice_in_dim(value_grads, value_term, start, 0)
            return (query_grad, key_grads, value_grads)

        return lax.cond(start < row_limit, grad_live, lambda state: state, carry)

    grad_init = (
        jnp.zeros((count, KVH, groups, HD), F32),
        jnp.zeros((length, KVH, HD), F32),
        jnp.zeros((length, KVH, HD), F32),
    )
    query_grad, key_grads, value_grads = lax.fori_loop(0, num_blocks, grad_step, grad_init)
    kv_part = jnp.concatenate(
        [(key_grads * scale).astype(BF).reshape(length, 256), value_grads.astype(BF).reshape(length, 256)],
        axis=1,
    )
    kv_grad = scatter_keys(kv_part.reshape(4, 4, 2, TOK, 512))
    query_pre = rotate_back((query_grad * scale).reshape(count, H, HD), cosine, sine).reshape(
        count, HQ
    )
    key_pre = rotate_back(kv_grad[0].reshape(count, KVH, HD), cosine, sine).reshape(count, KVH * HD)
    qkv_grad = jnp.concatenate([query_pre, key_pre, kv_grad[1]], axis=1).astype(BF)
    normed_one_grad = dot(qkv_grad, w_qkv, (1, 0))
    scaled_one = gain_one * normed_one_grad
    gain_one_grad = jnp.sum(normed_one_grad * inputs * factor_one, axis=0)
    input_grad = (
        middle_grad
        + factor_one * scaled_one
        - inputs * factor_one**3 * jnp.mean(scaled_one * inputs, axis=-1, keepdims=True)
    )

    qkv_part = dot(qkv_grad, normed_one, (0, 0)).astype(BF)
    out_part = dot(attended_low, branch_grad, (0, 0)).astype(BF)
    bias_part = jnp.sum(qkv_grad.astype(F32), axis=0).astype(BF)
    small_part = jnp.concatenate(
        [
            bias_part.reshape(128, 16),
            gain_one_grad.astype(BF).reshape(128, 12),
            gain_two_grad.astype(BF).reshape(128, 12),
            jnp.zeros((128, D - 40), BF),
        ],
        axis=1,
    )
    out_part = jnp.concatenate(
        [out_part.reshape(128, 12, D), small_part[:, None], jnp.zeros((128, 3, D), BF)], axis=1
    )
    gate_part = dot(gate_grad, rows_two, (0, 0)).astype(BF)
    up_part = dot(upward_grad, rows_two, (0, 0)).astype(BF)
    down_part = dot(hidden, cot_rows, (0, 0)).astype(BF)
    lead = lead_of(AXES) + (16, D)
    ffn_lead = lead_of(FFN_DIMS) + (ROWS, D)
    qkv_sum, out_sum, gate_sum, up_sum, down_sum = scatter_weight_grads(
        qkv_part.reshape(lead),
        out_part.reshape(lead),
        gate_part.reshape(ffn_lead),
        up_part.reshape(ffn_lead),
        down_part.reshape(ffn_lead),
    )
    units = gate_weight.shape[0]
    return (
        layer_out[None],
        input_grad[None],
        qkv_sum,
        out_sum[12, :16],
        out_sum[:12],
        out_sum[12, 16:40].reshape(2, 12),
        gate_sum[:units],
        up_sum[:units],
        down_sum[:units],
    )


def solution(mesh):
    fine = Mesh(mesh.devices.reshape(tuple(SIZE[a] for a in AXES)), AXES)
    dp, ctx = ("zl", "c"), ("y", "x", "zh")
    in_specs = (
        P(dp, ctx, None),
        P(AXES, None),
        P(AXES),
        P(AXES, None),
        P(None, AXES),
        P(AXES, None),
        P(AXES, None),
        P(AXES, None),
        P(dp, None),
        P(dp, ctx, None),
    )
    out_specs = (
        P(dp, ctx, None),
        P(dp, ctx, None),
        P(AXES, None),
        P(AXES),
        P(AXES, None),
        P(None, AXES),
        P(AXES, None),
        P(AXES, None),
        P(AXES, None),
    )
    return jax.shard_map(local, mesh=fine, in_specs=in_specs, out_specs=out_specs, check_vma=False)
```

time: 3940 us -> 788 us (0.20)
  waiting for transfers between devices: 2940 us -> 0 us
  Pallas kernels: 0 us -> 548 us
  blocking collectives: 456 us -> 0 us
  matrix products: 218 us -> 93.8 us
  starting transfers between devices: 94.9 us -> 0 us
  local copies, waits for them, and re-layouts: 190 us -> 106 us
    all_gather x11 -> x0, waiting for transfers between devices: 2600 us -> none  [the longest x1 352 us: local(): lax.all_gather(normed_two, ('dp', 'ctx'), axis=0, tiled=True)]
    pallas_call x0 -> x6, Pallas kernels: none -> 548 us  [the longest x1 159 us: gather_weights(): pl.pallas_call(weights_kernel, out_shape=(every, every, ffn, ffn, ffn, ro...]
    all_gather x1 -> x0, blocking collectives: 317 us -> none  [local(): lax.all_gather(norm_gains, ('dp', 'ctx'), axis=1, tiled=True)]
    unnamed x15 -> x0, waiting for transfers between devices: 279 us -> none
    unnamed x2 -> x0, blocking collectives: 139 us -> none
    unnamed x68, local copies, waits for them, and re-layouts: 140 us -> 4.55 us
    dot_general x19, matrix products: 213 us -> 88.9 us  [the longest x15 82.5 us: dot(): lax.dot_general(a, b, ((dims[:1], dims[1:]), ((), ())), preferred_element...]
    all_to_all x5 -> x0, starting transfers between devices: 94.2 us -> none  [the longest x1 70 us: local(): lax.all_to_all(attended_low, ('dp', 'ctx'), split_axis=1, concat_axis=0,...]
  transfers between devices with their start and end apart: 18 -> 0, of which waited for: 16 -> 0; matrix products, arithmetic and copies ran while one was open for 7% -> 0% of each run, Pallas kernels for 0% -> 0%
where the time goes in v1:
time: 788 us; the launch traced here: 780 us
  Pallas kernels  548 us (70%)
  local copies, waits for them, and re-layouts  106 us (13%)
  matrix products  93.8 us (12%)
  other arithmetic  29.9 us (4%)
    pallas_call x1, Pallas kernels, gather_weights(): pl.pallas_call(weights_kernel, out_shape=(every, every, ffn, ffn, ffn, ro...  159 us
    pallas_call x1, Pallas kernels, scatter_keys(): pl.pallas_call(keys_scatter_kernel, out_shape=jax.ShapeDtypeStruct((2, TO...  138 us
    pallas_call x1, Pallas kernels, scatter_weight_grads(): pl.pallas_call(weight_grads_kernel, out_shape=(attn, attn, ffn, ffn, ffn)...  119 us
    dot_general x15, matrix products, dot(): lax.dot_general(a, b, ((dims[:1], dims[1:]), ((), ())), preferred_element...  82.5 us
    pallas_call x1, Pallas kernels, gather_keys(): pl.pallas_call(keys_kernel, out_shape=jax.ShapeDtypeStruct((4, 4, 2, TOK,...  47.1 us
    pallas_call x1, Pallas kernels, scatter_rows(): pl.pallas_call(rows_scatter_kernel, out_shape=(one, one), in_specs=[ANY]...  44 us
    pallas_call x1, Pallas kernels, gather_rows(): pl.pallas_call(rows_kernel, out_shape=jax.ShapeDtypeStruct((4, 2, TOK, D)...  40.1 us
    convert_element_type x1, local copies, waits for them, and re-layouts, local(): (key_grads * scale).astype(BF).reshape(length, 256)  18.1 us

profile of v1, /device:TPU:0, one launch (start us, length us, event | category | flops | bytes accessed | tf_op | source)
XLA Modules:
  0.0 780.4 jit_solution(15511016392588285850)
XLA Ops:
  4.7 1.5 maximum_maximum_fusion.1.refs_1_
  6.2 1.6 pad.10.refs_2_
  7.9 1.6 pad.11.refs_3_
  9.5 1.6 pad.12.refs_4_
  11.1 159.4 %shard_map.169 = (bf16[2,2,4,4,2,16,1536]{6,5,4,3,2,1,0:T(8,128)(2,1)}, bf16[2,2,4,4,2,16,1536]{6,5,4,3,2,1,0:T(8,128)(2,1)}, bf16[2,4,2,80,1536]{4,3,2,1,0:T(8,...) custom-call(bf16[16,1536]{1,0:T(8,128)(2,1)} %refs_0_.1, ...), custom_call_target="tpu_custom_call" | custom-call | tf_op jit(solution)/shard_map/pallas_call | solution.py:161
  170.6 1.2 fusion.88
  171.9 1.2 fusion.87
  173.9 4.9 convolution_add_fusion.1
  180.3 47.1 %shard_map.170 = bf16[4,4,2,128,512]{4,3,2,1,0:T(8,128)(2,1)} custom-call(bf16[128,512]{1,0:T(8,128)(2,1)} %pad_maximum_fusion.3.block), custom_call_target="tpu_custom_call" | custom-call | tf_op jit(solution)/shard_map/pallas_call | solution.py:191
  227.4 7.4 reshape.334
  234.9 4.7 fusion.94
  239.6 2.5 copy_bitcast_fusion
  243.0 2.3 copy.67
  245.3 1.2 slice_negate_fusion.1
  246.5 1.2 fusion.72
  248.6 3.6 while.51
  248.6 3.2 conditional.9
  249.6 1.6 fusion.6
  252.3 3.9 copy.98
  256.3 3.4 while.52
  256.3 3.0 conditional.10
  257.3 2.0 fusion.16
  260.6 8.2 %reshape.337 = bf16[1536,1536]{1,0:T(8,128)(2,1)} reshape(bf16[128,12,1536]{2,1,0:T(8,128)(2,1)} %bitcast.251) | data formatting | bytes 9437184 | tf_op jit(solution)/shard_map/reshape | solution.py:506
  268.8 3.2 multiply_reduce_fusion.3
  274.1 40.1 %shard_map.171 = bf16[4,2,128,1536]{3,2,1,0:T(8,128)(2,1)} custom-call(bf16[128,1536]{1,0:T(8,128)(2,1)} %multiply_convert_fusion.4.block), custom_call_target="tpu_custom_call" | custom-call | tf_op jit(solution)/shard_map/pallas_call | solution.py:217
  314.3 7.5 fusion.98
  321.8 5.9 fusion.97
  327.8 9.7 %multiply_convert_fusion = (bf16[1024,1280]{1,0:T(8,128)(2,1)S(1)}, bf16[1024,1280]{1,0:T(8,128)(2,1)}, bf16[1024,1280]{1,0:T(8,128)(2,1)}) fusion(f32[1024,1280]{1,0:T(8,128)} %fusion.97, f32[1024,1280]{1,0:T(8,128)S(1)} %fusion.98, bf16[1024,1536]{1,0:T(8,128)(2,1)S(1)} %bitcast.285, bf16[1280,1536]{1,0:T(8,128)(2,1)S(1)} %bitcast.279), kind=kOutput, calls=%fused_computation.68 | convolution fusion | flops 4047503360 | bytes 25427968 | tf_op jit(solution)/shard_map/dot_general | solution.py:467
  337.4 6.9 fusion.99
  344.4 5.7 add_convert_fusion
  350.1 4.4 convolution_convert_fusion.5
  354.6 44.0 %shard_map.172 = (f32[128,1536]{1,0:T(8,128)S(1)}, f32[128,1536]{1,0:T(8,128)S(1)}) custom-call(bf16[4,2,128,1536]{3,2,1,0:T(8,128)(2,1)S(1)} %bitcast.243, bf16[4,2,128,1536]{3,2,1,0:T(8,128)(2,1)} %bitcast.264), custom_call_target="tpu_custom_call" | custom-call | tf_op jit(solution)/shard_map/pallas_call | solution.py:320
  399.9 3.5 convolution_convert_fusion.4
  403.4 8.1 %concatenate.81 = bf16[2,2,4,4,2,12,1536]{6,5,4,3,2,1,0:T(8,128)(2,1)} reshape(bf16[1536,1536]{1,0:T(8,128)(2,1)} %convolution_convert_fusion.4) | data formatting | bytes 9437184 | tf_op jit(solution)/shard_map/concatenate | solution.py:683
  411.5 4.0 convolution_convert_fusion.6
  416.1 1.5 broadcast_convert_fusion
  417.6 2.2 broadcast.156
  419.9 9.3 %while.53 = (s32[]{:T(128)}, f32[128,2,6,128]{0,3,2,1:T(8,128)S(1)}, f32[4096,2,128]{2,0,1:T(8,128)}, bf16[4096,2,128]{2,0,1:T(8,128)(2,1)}, s32[]{:T(128)}, /*i...) while((s32[]{:T(128)}, ...), condition=%wide.region_20.21_spmd.clone, body=%wide.region_17.20_spmd.clone.sunk | while | flops 1014891136 | bytes 19364760 | solution.py:651
  420.1 8.8 %conditional.11 = ((f32[128,2,6,128]{0,3,2,1:T(8,128)S(1)}, f32[4096,2,128]{2,0,1:T(8,128)}, bf16[4096,2,128]{2,0,1:T(8,128)(2,1)})) conditional(s32[]{:T(128)} %convert_element_type.331, (f32[128,2,6,128]{0,3,2,1:T(8,128)S(1)}, f32[4096,2,128]{2,0,1:T(8,128)}, bf16[4096,2,128]{2,0,1:T(8,128)(2,1)}) %tuple.149, (s32[]{:T(128)}, ...), branch_computations={%region_18.18_spmd, %region_19.19_spmd} | conditional | flops 1014891136 | bytes 19363938 | solution.py:644
  421.1 1.5 fusion.43
  422.6 2.0 fusion.28
  424.7 1.4 fusion.36
  426.1 1.4 fusion.35
  427.5 1.4 fusion.40
  429.5 1.9 copy-done
  431.9 18.1 %copy.76 = bf16[4096,2,128]{2,1,0:T(2,128)(2,1)} copy(bf16[4096,2,128]{2,0,1:T(8,128)(2,1)S(1)} %multiply_convert_fusion.3) | data formatting | bytes 4194304 | tf_op jit(solution)/shard_map/convert_element_type | solution.py:653
  450.0 4.4 concatenate.75
  454.4 5.8 copy.77
  460.2 4.4 concatenate.76
  464.5 2.6 pad_maximum_fusion.source
  467.2 138.2 %shard_map.173 = f32[2,128,256]{2,1,0:T(8,128)S(1)} custom-call(bf16[4,4,2,128,512]{4,3,2,1,0:T(8,128)(2,1)S(1)} %pad_maximum_fusion.source), custom_call_target="tpu_custom_call" | custom-call | tf_op jit(solution)/shard_map/pallas_call | solution.py:358
  606.7 4.0 fusion.68
  610.9 1.5 broadcast_in_dim.75
  612.4 6.6 concatenate.83
  619.1 8.9 %maximum_maximum_fusion.refs_1_ = bf16[2,2,4,4,2,16,1536]{6,5,4,3,2,1,0:T(8,128)(2,1)} fusion(bf16[2,2,4,4,2,1,1536]{6,5,4,3,2,1,0:T(2,128)(2,1)} %concatenate.83, bf16[2,2,4,4,2,12,1536]{6,5,4,3,2,1,0:T(8,128)(2,1)} %concatenate.81, bf16[16]{0:T(256)(128)(2,1)S(1)} %copy-done.20), kind=kLoop, calls=%fused_computation.66 | loop fusion | flops 18874368 | bytes 11403296 | tf_op jit(solution)/shard_map/concatenate | solution.py:683
  628.0 5.9 convolution_convert_fusion.2
  633.9 5.9 convolution_convert_fusion.1
  639.8 4.5 convolution_convert_fusion.3
  644.3 6.3 convolution_convert_fusion
  650.6 118.8 %shard_map.174 = (f32[16,1536]{1,0:T(8,128)}, f32[16,1536]{1,0:T(8,128)}, f32[80,1536]{1,0:T(8,128)}, f32[80,1536]{1,0:T(8,128)}, f32[80,1536]{1,0:T(8,128)}) custom-call(bf16[2,2,4,4,2,16,1536]{6,5,4,3,2,1,0:T(8,128)(2,1)} %bitcast.244, bf16[2,2,4,4,2,16,1536]{6,5,4,3,2,1,0:T(8,128)(2,1)} %maximum_maximum_fusion.refs_1_, ...), custom_call_target="tpu_custom_call" | custom-call | tf_op jit(solution)/shard_map/pallas_call | solution.py:419
  769.4 1.8 slice.100
  771.3 1.8 slice.101
  773.1 1.8 slice.99
  776.3 1.2 slice_bitcast_fusion
  (197 shorter events, 23.1 us)
Async XLA Ops:
  0.6 172.5 %copy-start.1 = (bf16[1,128,1536]{2,1,0:T(8,128)(2,1)S(1)}, bf16[1,128,1536]{2,1,0:T(8,128)(2,1)}, u32[]{:S(2)}) copy-start(bf16[1,128,1536]{2,1,0:T(8,128)(2,1)} %param.22) | copy-start | bytes 1179652
  3.1 176.1 %copy-start.11 = (f32[128,128]{1,0:T(8,128)}, f32[128,128]{1,0:T(8,128)S(1)}, u32[]{:S(2)}) copy-start(f32[128,128]{1,0:T(8,128)S(1)} %copy.64) | copy-start | bytes 196612
  3.2 167.4 %copy-start.19 = (bf16[16]{0:T(256)(128)(2,1)}, bf16[16]{0:T(256)(128)(2,1)S(1)}, u32[]{:S(2)}) copy-start(bf16[16]{0:T(256)(128)(2,1)S(1)} %pad.35.clone) | copy-start | bytes 100
  171.9 7.0 copy-start.13
  173.9 5.0 copy-start.17
  178.9 48.5 %copy-start.4 = (f32[128,2048]{1,0:T(8,128)}, f32[128,2048]{1,0:T(8,128)S(1)}, u32[]{:S(2)}) copy-start(f32[128,2048]{1,0:T(8,128)S(1)} %convolution_add_fusion.1) | copy-start | bytes 3145732
  179.6 55.3 %copy-start.9 = (f32[128,2,128]{2,1,0:T(2,128)}, f32[128,2,128]{2,1,0:T(2,128)S(1)}, u32[]{:S(2)}) copy-start(f32[128,2,128]{2,1,0:T(2,128)S(1)} %mul.326) | copy-start | bytes 393220
  239.6 2.5 copy-start.5
  259.7 0.9 copy-start.2
  314.3 7.5 copy-start.6
  314.3 7.5 copy-start.24
  321.8 6.0 copy-start.22
  321.8 6.0 copy-start.25
  337.4 7.0 copy-start.27
  337.4 7.0 copy-start.23
  344.4 5.7 copy-start.30
  354.6 44.2 %copy-start.8 = (bf16[1,128,1536]{2,1,0:T(8,128)(2,1)S(1)}, bf16[1,128,1536]{2,1,0:T(8,128)(2,1)}, u32[]{:S(2)}) copy-start(bf16[1,128,1536]{2,1,0:T(8,128)(2,1)} %param.31) | copy-start | bytes 1179652
  411.5 4.3 copy-start.3
  429.2 2.2 copy-start
  467.2 138.3 %copy-start.12 = (f32[128,128]{1,0:T(8,128)S(1)}, f32[128,128]{1,0:T(8,128)}, u32[]{:S(2)}) copy-start(f32[128,128]{1,0:T(8,128)} %copy-done.11) | copy-start | bytes 196612
  467.2 138.8 %copy-start.10 = (f32[128,2,128]{2,1,0:T(2,128)S(1)}, f32[128,2,128]{2,1,0:T(2,128)}, u32[]{:S(2)}) copy-start(f32[128,2,128]{2,1,0:T(2,128)} %copy-done.9) | copy-start | bytes 393220
  467.2 139.5 %copy-start.14 = (f32[1536]{0:T(1024)S(1)}, f32[1536]{0:T(1024)}, u32[]{:S(2)}) copy-start(f32[1536]{0:T(1024)} %copy-done.13) | copy-start | bytes 18436
  467.2 139.5 %copy-start.18 = (f32[128]{0:T(128)S(1)}, f32[128]{0:T(128)}, u32[]{:S(2)}) copy-start(f32[128]{0:T(128)} %copy-done.17) | copy-start | bytes 1540
  606.7 12.4 %copy-start.20 = (bf16[16]{0:T(256)(128)(2,1)S(1)}, bf16[16]{0:T(256)(128)(2,1)}, u32[]{:S(2)}) copy-start(bf16[16]{0:T(256)(128)(2,1)} %copy-done.19) | copy-start | bytes 100
  619.1 8.9 %copy-start.7 = (bf16[4,2,128,1536]{3,2,1,0:T(8,128)(2,1)S(1)}, bf16[4,2,128,1536]{3,2,1,0:T(8,128)(2,1)}, u32[]{:S(2)}) copy-start(bf16[4,2,128,1536]{3,2,1,0:T(8,128)(2,1)} %shard_map.171) | copy-start | bytes 9437188
  619.1 8.9 %copy-start.29 = (bf16[1024,1280]{1,0:T(8,128)(2,1)S(1)}, bf16[1024,1280]{1,0:T(8,128)(2,1)}, u32[]{:S(2)}) copy-start(bf16[1024,1280]{1,0:T(8,128)(2,1)} %get-tuple-element.971) | copy-start | bytes 7864324
  628.0 5.9 copy-start.28
  639.8 4.5 copy-start.26
  639.8 4.5 copy-start.31
  650.6 126.9 %copy-start.21 = (f32[128]{0:T(128)S(1)}, f32[128]{0:T(128)}, u32[]{:S(2)}) copy-start(f32[128]{0:T(128)} %get-tuple-element.987) | copy-start | bytes 1540
  769.4 9.2 %copy-start.16 = (f32[16,1536]{1,0:T(8,128)S(1)}, f32[16,1536]{1,0:T(8,128)}, u32[]{:S(2)}) copy-start(f32[16,1536]{1,0:T(8,128)} %get-tuple-element.1345) | copy-start | bytes 294916
  769.4 9.9 %copy-start.15 = (f32[16,1536]{1,0:T(8,128)S(1)}, f32[16,1536]{1,0:T(8,128)}, u32[]{:S(2)}) copy-start(f32[16,1536]{1,0:T(8,128)} %get-tuple-element.715) | copy-start | bytes 294916

commit v2 on v1

v2 whole, which is shorter than its diff:
```python
import math

import jax
import jax.numpy as jnp
from jax import lax
from jax.experimental import pallas as pl
from jax.experimental.pallas import tpu as pltpu
from jax.sharding import Mesh
from jax.sharding import PartitionSpec as P

H = 12
KVH = 2
HD = 128
HQ = 1536
D = 1536
TOK = 128
ROWS = 80

norm_eps = 1e-06
rope_base = 1000000.0
doc_kinds = 3

AXES = ("zl", "c", "y", "x", "zh")
SIZE = {"zl": 2, "c": 2, "y": 4, "x": 4, "zh": 2}
PARTS_OF = {"z": ("zl", "zh"), "x": ("x",), "y": ("y",), "c": ("c",), "zh": ("zh",)}
REACH = {"z": (1, 2, 3), "x": (1, 2, 3), "y": (1, 2, 3), "c": (1,), "zh": (1,)}
BF = jnp.bfloat16
F32 = jnp.float32
ANY = pl.BlockSpec(memory_space=pl.ANY)
VMEM = pl.BlockSpec(memory_space=pltpu.VMEM)


def here():
    return {a: lax.axis_index(a) for a in AXES}


def peer(me, axis, k):
    to = dict(me)
    if axis == "z":
        z = lax.rem(me["zh"] * 2 + me["zl"] + k, 4)
        to["zl"], to["zh"] = lax.rem(z, 2), lax.div(z, 2)
    else:
        to[axis] = lax.rem(me[axis] + k, SIZE[axis])
    return to


def device_id(at):
    return tuple(at[a] for a in AXES)


def place(dims, at, whole, tail=()):
    return tuple(slice(None) if d in whole else at[d] for d in dims) + tuple(tail)


class Links:
    def __init__(self, me, send, recv):
        self.me, self.send, self.recv, self.used = me, send, recv, 0

    def copy(self, src, dst, axis, k):
        i = self.used
        self.used += 1
        c = pltpu.make_async_remote_copy(
            src_ref=src,
            dst_ref=dst,
            send_sem=self.send.at[i],
            recv_sem=self.recv.at[i],
            device_id=device_id(peer(self.me, axis, k)),
            device_id_type=pl.DeviceIdType.MESH,
        )
        c.start()
        return c


def greet(me, axes):
    barrier = pltpu.get_barrier_semaphore()
    count = 0
    for axis in axes:
        for k in REACH[axis]:
            pl.semaphore_signal(
                barrier,
                inc=1,
                device_id=device_id(peer(me, axis, k)),
                device_id_type=pl.DeviceIdType.MESH,
            )
            count += 1
    pl.semaphore_wait(barrier, count)


def gather_stream(links, block, buf, dims, tail, order):
    me = links.me
    whole = ()
    for n, axis in enumerate(order):
        mine = place(dims, me, whole, tail)
        src = block if n == 0 else buf.at[mine]
        copies = [links.copy(src, buf.at[mine], axis, k) for k in REACH[axis]]
        yield
        for c in copies:
            c.wait()
        whole = whole + PARTS_OF[axis]


def run_streams(streams):
    live = list(streams)
    while live:
        live = [s for s in live if next(s, live) is not live]


def step(streams):
    for s in streams:
        next(s, None)


def count_gather(orders):
    return sum(len(REACH[a]) for order in orders for a in order)


THIRDS = tuple((slice(None), slice(512 * i, 512 * (i + 1))) for i in range(3))
ORDERS = (("x", "y", "z"), ("y", "z", "x"), ("z", "x", "y"))
HALVES = tuple((slice(None), slice(768 * i, 768 * (i + 1))) for i in range(2))
FFN_ORDERS = (("y", "z"), ("z", "y"))
FFN_DIMS = ("zl", "y", "zh")
ROW_DIMS = ("x", "c")
KV_DIMS = ("y", "x", "zh")


def weights_kernel(qkv, out, small, qkv_all, out_all, small_all, send, recv, local):
    me = here()
    links = Links(me, send, recv)
    own = []
    pairs = ((qkv, qkv_all), (out, out_all), (small, small_all))
    for i, (a, b) in enumerate(pairs):
        own.append(pltpu.make_async_copy(a, b.at[place(AXES, me, ())], local.at[i]))
        own[-1].start()
    greet(me, ("x", "y", "z", "c"))
    for c in own:
        c.wait()
    streams = []
    for block, buf in pairs[:2]:
        for order, tail in zip(ORDERS, THIRDS, strict=True):
            streams.append(
                gather_stream(links, block.at[tail], buf, AXES, tail, order + ("c",))
            )
    streams.append(gather_stream(links, small, small_all, AXES, (), ORDERS[0] + ("c",)))
    run_streams(streams)


def gather_weights(qkv, out, small):
    every = jax.ShapeDtypeStruct(lead_of(AXES) + (16, D), BF)
    smalls = jax.ShapeDtypeStruct(lead_of(AXES) + (16, 128), BF)
    copies = 2 * count_gather([o + ("c",) for o in ORDERS]) + count_gather([ORDERS[0] + ("c",)])
    return pl.pallas_call(
        weights_kernel,
        out_shape=(every, every, smalls),
        in_specs=[ANY] * 3,
        out_specs=(ANY,) * 3,
        scratch_shapes=[
            pltpu.SemaphoreType.DMA((copies,)),
            pltpu.SemaphoreType.DMA((copies,)),
            pltpu.SemaphoreType.DMA((3,)),
        ],
        compiler_params=pltpu.CompilerParams(collective_id=1, has_side_effects=True),
    )(qkv, out, small)


GROUP = H // KVH
GQ = GROUP * TOK
KEYS = 512
SCALE = HD**-0.5
TO_LOG2 = SCALE * math.log2(math.e)


def head(h):
    return slice(128 * h, 128 * (h + 1))


def turned(v):
    return pltpu.roll(v, 64, 1)


def key_blocks():
    ctx = lax.axis_index("y") * 8 + lax.axis_index("x") * 2 + lax.axis_index("zh")
    return lax.div(ctx, 4) + 1, ctx * TOK


def key_block_of(ref, b, cols):
    return ref[lax.div(b, 2), pl.ds(lax.rem(b, 2) * 2, 2), :, :, cols].reshape(KEYS, HD)


def allowed_keys(b, first, row):
    key = b * KEYS + lax.broadcasted_iota(jnp.int32, (KEYS, GQ), 0)
    query = row + lax.rem(lax.broadcasted_iota(jnp.int32, (1, GQ), 1), TOK)
    return (key <= query) & (key >= first)


def mm(a, b, contract):
    return lax.dot_general(
        a, b, ((contract[:1], contract[1:]), ((), ())), preferred_element_type=F32
    )


def attend_group(g, kv, qs, first, row, blocks, acc, stats):
    acc[...] = jnp.zeros_like(acc)
    stats[0:1] = jnp.full((1, GQ), -1e30, F32)
    stats[1:2] = jnp.zeros((1, GQ), F32)

    def body(b, carry):
        keys = key_block_of(kv, b, head(g))
        values = key_block_of(kv, b, head(2 + g))
        raw = mm(keys, qs[g], (1, 1)) * TO_LOG2
        raw = jnp.where(allowed_keys(b, first, row), raw, -1e30)
        old = stats[0:1]
        top = jnp.maximum(old, jnp.max(raw, axis=0, keepdims=True))
        probs = jnp.exp2(raw - top)
        shrink = jnp.exp2(old - top)
        stats[0:1] = top
        stats[1:2] = stats[1:2] * shrink + jnp.sum(probs, axis=0, keepdims=True)
        acc[...] = acc[...] * shrink + mm(values.T, probs.astype(BF), (1, 0))
        return carry

    lax.fori_loop(0, blocks, body, 0)


def attend_kernel(*refs):
    qkv, cosine, sine, first_ref, spread, gate, up, down, cot = refs[:9]
    kv, queries, attended, slots, lse = refs[9:14]
    gate_all, up_all, down_all, cot_all = refs[14:18]
    block, qs, acc, stats, send, recv, local = refs[18:]
    me = here()
    links = Links(me, send, recv)
    own = []
    pairs = (
        (gate, gate_all, FFN_DIMS),
        (up, up_all, FFN_DIMS),
        (down, down_all, FFN_DIMS),
        (cot, cot_all, ROW_DIMS),
    )
    for i, (a, b, dims) in enumerate(pairs):
        own.append(pltpu.make_async_copy(a, b.at[place(dims, me, ())], local.at[i]))
        own[-1].start()
    cos, sin = cosine[...], sine[...]
    for g in range(KVH):
        part = qkv[:, head(H + g)]
        block[:, head(g)] = (part * cos + turned(part) * sin).astype(BF)
        block[:, head(2 + g)] = qkv[:, head(H + 2 + g)].astype(BF)
    own.append(pltpu.make_async_copy(block, kv.at[place(KV_DIMS, me, ())], local.at[4]))
    own[-1].start()
    greet(me, ("zh", "x", "y", "z", "c"))
    keys = []
    for half, order in enumerate((("zh", "x", "y"), ("zh", "y", "x"))):
        tail = (slice(None), slice(256 * half, 256 * (half + 1)))
        keys.append(gather_stream(links, block.at[tail], kv, KV_DIMS, tail, order))
    weights = []
    for a, b, _ in pairs[:3]:
        for order, tail in zip(FFN_ORDERS, HALVES, strict=True):
            weights.append(gather_stream(links, a.at[tail], b, FFN_DIMS, tail, order))
    rows = [gather_stream(links, cot, cot_all, ROW_DIMS, (), ("x", "c"))]
    step(keys)
    step(weights)
    for c in own:
        c.wait()
    step(keys)
    for h in range(H):
        part = qkv[:, head(h)]
        turned_q = (part * cos + turned(part) * sin).astype(BF)
        queries[:, head(h)] = turned_q
        qs[h // GROUP, (h % GROUP) * TOK : (h % GROUP + 1) * TOK, :] = turned_q
    step(keys)
    step(weights)
    step(rows)
    step(keys)
    blocks, row = key_blocks()
    first = first_ref[0:1]
    for g in range(KVH):
        attend_group(g, kv, qs, first, row, blocks, acc, stats)
        total = stats[1:2]
        lse[g] = jnp.broadcast_to(stats[0:1] + jnp.log2(total), (8, GQ))
        acc[...] = acc[...] / total
        for i in range(GROUP):
            attended[:, head(GROUP * g + i)] = acc[:, head(i)].T
        step(rows)
    for i in range(4):
        part = attended[:, 384 * i : 384 * (i + 1)].astype(BF)
        slots[:, 512 * i : 512 * (i + 1)] = mm(part, spread[...], (1, 0)).astype(BF)
    step(rows)
    step(weights)


def attend(qkv, cosine, sine, first, spread, gate, up, down, cot):
    ffn = jax.ShapeDtypeStruct(lead_of(FFN_DIMS) + (ROWS, D), BF)
    rows = jax.ShapeDtypeStruct(lead_of(ROW_DIMS) + (TOK, D), BF)
    copies = count_gather([("zh", "x", "y"), ("zh", "y", "x"), ("x", "c")])
    copies += 3 * count_gather(FFN_ORDERS)
    return pl.pallas_call(
        attend_kernel,
        out_shape=(
            jax.ShapeDtypeStruct(lead_of(KV_DIMS) + (TOK, 512), BF),
            jax.ShapeDtypeStruct((TOK, HQ), BF),
            jax.ShapeDtypeStruct((TOK, HQ), F32),
            jax.ShapeDtypeStruct((TOK, 2048), BF),
            jax.ShapeDtypeStruct((KVH, 8, GQ), F32),
            ffn,
            ffn,
            ffn,
            rows,
        ),
        in_specs=[VMEM] * 5 + [ANY] * 4,
        out_specs=(VMEM,) * 5 + (ANY,) * 4,
        scratch_shapes=[
            pltpu.VMEM((TOK, 512), BF),
            pltpu.VMEM((KVH, GQ, HD), BF),
            pltpu.VMEM((HD, GQ), F32),
            pltpu.VMEM((8, GQ), F32),
            pltpu.SemaphoreType.DMA((copies,)),
            pltpu.SemaphoreType.DMA((copies,)),
            pltpu.SemaphoreType.DMA((5,)),
        ],
        compiler_params=pltpu.CompilerParams(
            collective_id=2, has_side_effects=True, vmem_limit_bytes=48 * 2**20
        ),
    )(qkv, cosine, sine, first, spread, gate, up, down, cot)


def grad_group(g, kv, qs, gs, lse, delta, first, row, blocks, query_grad, kv_grad):
    query_grad[...] = jnp.zeros_like(query_grad)

    def body(b, carry):
        at = (lax.div(b, 2), pl.ds(lax.rem(b, 2) * 2, 2), slice(None), slice(None))
        keys = key_block_of(kv, b, head(g))
        values = key_block_of(kv, b, head(2 + g))
        raw = mm(keys, qs[g], (1, 1)) * TO_LOG2
        probs = jnp.where(allowed_keys(b, first, row), jnp.exp2(raw - lse), 0.0)
        prob_grad = mm(values, gs[g], (1, 1))
        score_grad = (probs * (prob_grad - delta)).astype(BF)
        key_term = mm(score_grad, qs[g], (1, 0)) * SCALE
        value_term = mm(probs.astype(BF), gs[g], (1, 0))
        kv_grad[at + (head(g),)] = key_term.astype(BF).reshape(2, 2, TOK, HD)
        kv_grad[at + (head(2 + g),)] = value_term.astype(BF).reshape(2, 2, TOK, HD)
        query_grad[...] += mm(keys.T, score_grad, (1, 0))
        return carry

    lax.fori_loop(0, blocks, body, 0)


FIRST_STAGE = (("y",), ("z",))
LAST_STAGE = (("z",), ("y",))


def attend_back_kernel(*refs):
    kv, queries, attended, grad_slots, lse, first_ref, cosine, sine, spread = refs[:9]
    parts = refs[9:12]
    qkv_grad = refs[12]
    sums = refs[13:19]
    qs, gs, delta, query_grad, kv_grad, kv_out, send, recv, local = refs[19:28]
    scratch = refs[28:]
    me = here()
    links = Links(me, send, recv)
    greet(me, ("zh", "x", "y", "z"))
    weights = []
    for i in range(6):
        order, tail = FIRST_STAGE[i % 2], HALVES[i % 2]
        weights.append(
            scatter_stream(
                links, local.at[i], parts[i // 2], FFN_DIMS, tail, order, scratch[2 * i : 2 * i + 2], sums[i], ROWS, 16
            )
        )
    step(weights)
    blocks, row = key_blocks()
    first = first_ref[0:1]
    for i in range(4):
        part = mm(grad_slots[:, 512 * i : 512 * (i + 1)], spread[...], (1, 1))
        for j in range(3):
            h = 3 * i + j
            one = part[:, head(j)]
            gs[h // GROUP, (h % GROUP) * TOK : (h % GROUP + 1) * TOK, :] = one.astype(BF)
            both = (one * attended[:, head(h)]).T
            delta[h // GROUP : h // GROUP + 1, head(h % GROUP)] = jnp.sum(
                both, axis=0, keepdims=True
            )
            qs[h // GROUP, (h % GROUP) * TOK : (h % GROUP + 1) * TOK, :] = queries[:, head(h)]

    def clear(b, carry):
        at = (lax.div(b, 2), pl.ds(lax.rem(b, 2) * 2, 2))
        kv_grad[at] = jnp.zeros((2, 2, TOK, 512), BF)
        return carry

    lax.fori_loop(blocks, 8, clear, 0)
    cos, sin = cosine[...], sine[...]
    for g in range(KVH):
        grad_group(
            g, kv, qs, gs, lse[g, 0:1], delta[g : g + 1], first, row, blocks, query_grad, kv_grad
        )
        for i in range(GROUP):
            one = query_grad[:, head(i)].T * SCALE
            qkv_grad[:, head(GROUP * g + i)] = (one * cos - turned(one) * sin).astype(BF)
    keys = []
    for half, order in enumerate(KV_ORDERS):
        tail = (slice(None), slice(256 * half, 256 * (half + 1)))
        part = scratch[12 + 6 * half : 18 + 6 * half]
        keys.append(
            scatter_stream(links, None, kv_grad, KV_DIMS, tail, order, part, kv_out.at[half], TOK, 32)
        )
    step(keys)
    step(keys)
    step(keys)
    step(keys)
    for g in range(KVH):
        one = kv_out[0, :, head(g)]
        qkv_grad[:, head(H + g)] = (one * cos - turned(one) * sin).astype(BF)
        qkv_grad[:, head(H + 2 + g)] = kv_out[1, :, head(g)].astype(BF)
    step(weights)


def attend_back(kv, queries, attended, grad_slots, lse, first, cosine, sine, spread, parts):
    copies = count_gather(KV_ORDERS) + 3 * count_gather(FIRST_STAGE)
    scratch, sums = [], []
    for _ in range(3):
        for order in FIRST_STAGE:
            scratch += scatter_scratch(FFN_DIMS, order, ROWS, 768)
            sums.append(
                jax.ShapeDtypeStruct(lead_of(rest_of(FFN_DIMS, order[0])) + (ROWS, 768), BF)
            )
    for order in KV_ORDERS:
        scratch += scatter_scratch(KV_DIMS, order, TOK, 256)
    return pl.pallas_call(
        attend_back_kernel,
        out_shape=(jax.ShapeDtypeStruct((TOK, 2048), BF),) + tuple(sums),
        in_specs=[VMEM] * 9 + [ANY] * 3,
        out_specs=(VMEM,) * 7,
        scratch_shapes=[
            pltpu.VMEM((KVH, GQ, HD), BF),
            pltpu.VMEM((KVH, GQ, HD), BF),
            pltpu.VMEM((8, GQ), F32),
            pltpu.VMEM((HD, GQ), F32),
            pltpu.VMEM(lead_of(KV_DIMS) + (TOK, 512), BF),
            pltpu.VMEM((2, TOK, 256), F32),
            pltpu.SemaphoreType.DMA((copies,)),
            pltpu.SemaphoreType.DMA((copies,)),
            pltpu.SemaphoreType.DMA((6,)),
        ]
        + scratch,
        compiler_params=pltpu.CompilerParams(
            collective_id=5, has_side_effects=True, vmem_limit_bytes=60 * 2**20
        ),
    )(kv, queries, attended, grad_slots, lse, first, cosine, sine, spread, *parts)


def rows_kernel(block, buf, send, recv, local):
    me = here()
    links = Links(me, send, recv)
    own = pltpu.make_async_copy(block, buf.at[place(ROW_DIMS, me, ())], local)
    own.start()
    greet(me, ("x", "c"))
    own.wait()
    run_streams([gather_stream(links, block, buf, ROW_DIMS, (), ("x", "c"))])


def gather_rows(block):
    copies = count_gather([("x", "c")])
    return pl.pallas_call(
        rows_kernel,
        out_shape=jax.ShapeDtypeStruct((4, 2, TOK, D), BF),
        in_specs=[ANY],
        out_specs=ANY,
        scratch_shapes=[
            pltpu.SemaphoreType.DMA((copies,)),
            pltpu.SemaphoreType.DMA((copies,)),
            pltpu.SemaphoreType.DMA,
        ],
        compiler_params=pltpu.CompilerParams(collective_id=3, has_side_effects=True),
    )(block)


def lead_of(dims):
    return tuple(SIZE[d] for d in dims)


def rest_of(dims, axis):
    return tuple(d for d in dims if d not in PARTS_OF[axis])


def scatter_scratch(dims, order, rows, cols):
    shapes = []
    for axis in order:
        dims = rest_of(dims, axis)
        shapes.append(pltpu.VMEM((len(REACH[axis]),) + lead_of(dims) + (rows, cols), BF))
        shapes.append(pltpu.VMEM(lead_of(dims) + (rows, cols), BF))
    return shapes


def sum_blocks(own, arrived, out, lead, rows, step):
    count = 1
    for n in lead:
        count *= n
    per = rows // step
    parts = arrived.shape[0]

    def body(i, carry):
        block, row = lax.div(i, per), lax.rem(i, per)
        index = []
        for n in reversed(lead):
            index.append(lax.rem(block, n))
            block = lax.div(block, n)
        at = tuple(reversed(index)) + (pl.ds(pl.multiple_of(row * step, step), step),)
        total = own[at].astype(F32)
        for p in range(parts):
            total = total + arrived[(p,) + at].astype(F32)
        out[at] = total.astype(out.dtype)
        return carry

    lax.fori_loop(0, count * per, body, 0)


def scatter_stream(links, local, source, dims, tail, order, scratch, out, rows, step):
    me = links.me
    now = None
    for n, axis in enumerate(order):
        arrived, own = scratch[2 * n], scratch[2 * n + 1]
        gone = PARTS_OF[axis]
        keep = tuple(d for d in dims if d not in gone)
        end = tail if n == 0 else ()
        base = source if n == 0 else now
        copies = []
        for k in REACH[axis]:
            to = peer(me, axis, k)
            src = base.at[place(dims, to, keep, end)]
            copies.append(links.copy(src, arrived.at[k - 1], axis, k))
        held = base.at[place(dims, me, keep, end)]
        staged = n == 0 and local is not None
        if staged:
            mine = pltpu.make_async_copy(held, own, local)
            mine.start()
        yield
        if staged:
            mine.wait()
            held = own
        for c in copies:
            c.wait()
        target = out if n == len(order) - 1 else own
        sum_blocks(held, arrived, target, lead_of(keep), rows, step)
        now, dims = own, keep


def rows_scatter_kernel(first, second, out_a, out_b, send, recv, local, *scratch):
    me = here()
    links = Links(me, send, recv)
    greet(me, ("x", "c"))
    half = len(scratch) // 2
    run_streams(
        [
            scatter_stream(
                links, local.at[0], first, ROW_DIMS, (), ("c", "x"), scratch[:half], out_a, TOK, 16
            ),
            scatter_stream(
                links, local.at[1], second, ROW_DIMS, (), ("c", "x"), scratch[half:], out_b, TOK, 16
            ),
        ]
    )


def scatter_rows(first, second):
    copies = 2 * count_gather([("c", "x")])
    one = jax.ShapeDtypeStruct((TOK, D), F32)
    return pl.pallas_call(
        rows_scatter_kernel,
        out_shape=(one, one),
        in_specs=[ANY] * 2,
        out_specs=(VMEM,) * 2,
        scratch_shapes=[
            pltpu.SemaphoreType.DMA((copies,)),
            pltpu.SemaphoreType.DMA((copies,)),
            pltpu.SemaphoreType.DMA((2,)),
        ]
        + 2 * scatter_scratch(ROW_DIMS, ("c", "x"), TOK, D),
        compiler_params=pltpu.CompilerParams(
            collective_id=4, has_side_effects=True, vmem_limit_bytes=48 * 2**20
        ),
    )(first, second)


KV_ORDERS = (("y", "x", "zh"), ("x", "y", "zh"))
ALL_ORDERS = tuple(("c",) + o for o in ORDERS)


def weight_grads_kernel(*refs):
    qkv, out, small = refs[:3]
    parts = refs[3:9]
    qkv_out, out_out, small_out = refs[9:12]
    ffn_outs = refs[12:15]
    send, recv, local = refs[15:18]
    scratch = list(refs[18:])
    me = here()
    links = Links(me, send, recv)
    greet(me, ("x", "y", "z", "c"))
    streams = []

    def add(source, dims, order, tail, target, rows):
        n = 2 * len(order)
        part = [scratch.pop(0) for _ in range(n)]
        streams.append(
            scatter_stream(
                links, local.at[len(streams)], source, dims, tail, order, part, target, rows, 16
            )
        )

    for source, target in ((qkv, qkv_out), (out, out_out)):
        for order, tail in zip(ALL_ORDERS, THIRDS, strict=True):
            add(source, AXES, order, tail, target.at[tail], 16)
    add(small, AXES, ALL_ORDERS[0], (), small_out, 16)
    for i, source in enumerate(parts):
        order = LAST_STAGE[i % 2]
        dims = rest_of(FFN_DIMS, FIRST_STAGE[i % 2][0])
        add(source, dims, order, (), ffn_outs[i // 2].at[HALVES[i % 2]], ROWS)
    run_streams(streams)


def scatter_weight_grads(qkv, out, small, parts):
    copies = 2 * count_gather(ALL_ORDERS) + count_gather(ALL_ORDERS[:1])
    copies += 3 * count_gather(LAST_STAGE)
    scratch = []
    for _ in range(2):
        for order in ALL_ORDERS:
            scratch += scatter_scratch(AXES, order, 16, 512)
    scratch += scatter_scratch(AXES, ALL_ORDERS[0], 16, 128)
    for i in range(6):
        scratch += scatter_scratch(
            rest_of(FFN_DIMS, FIRST_STAGE[i % 2][0]), LAST_STAGE[i % 2], ROWS, 768
        )
    attn = jax.ShapeDtypeStruct((16, D), F32)
    ffn = jax.ShapeDtypeStruct((ROWS, D), F32)
    return pl.pallas_call(
        weight_grads_kernel,
        out_shape=(attn, attn, jax.ShapeDtypeStruct((16, 128), F32), ffn, ffn, ffn),
        in_specs=[ANY] * 9,
        out_specs=(VMEM,) * 6,
        scratch_shapes=[
            pltpu.SemaphoreType.DMA((copies,)),
            pltpu.SemaphoreType.DMA((copies,)),
            pltpu.SemaphoreType.DMA((13,)),
        ]
        + scratch,
        compiler_params=pltpu.CompilerParams(
            collective_id=6, has_side_effects=True, vmem_limit_bytes=60 * 2**20
        ),
    )(qkv, out, small, *parts)


def positions_of(documents):
    index = jnp.arange(documents.shape[0], dtype=jnp.int32)
    kinds = jnp.arange(doc_kinds, dtype=jnp.int32)
    counts = jnp.sum((documents[None, :] == kinds[:, None]).astype(jnp.int32), axis=1)
    starts = jnp.cumsum(counts) - counts
    first = jnp.sum(jnp.where(documents[:, None] == kinds[None, :], starts[None, :], 0), axis=1)
    return index - first


def rope_tables(position):
    half = HD // 2
    inverse = rope_base ** (-(jnp.arange(half, dtype=jnp.float32) * 2.0 / HD))
    angle = position.astype(jnp.float32)[:, None] * inverse[None, :]
    angle = jnp.concatenate([angle, angle], axis=1)
    return (jnp.cos(angle), jnp.sin(angle))


def dot(a, b, dims):
    return lax.dot_general(a, b, ((dims[:1], dims[1:]), ((), ())), preferred_element_type=F32)


def local(
    tokens_in,
    qkv_weight,
    qkv_bias,
    out_weight,
    norm_gains,
    gate_weight,
    up_weight,
    down_weight,
    doc_ids,
    cotangent,
):
    block_index = lax.axis_index("y") * 8 + lax.axis_index("x") * 2 + lax.axis_index("zh")
    inputs = tokens_in[0].astype(F32)
    documents = doc_ids[0]
    cot_low = cotangent[0]

    small = jnp.concatenate([qkv_bias, norm_gains.reshape(-1)])[None]
    small = jnp.pad(small, ((0, 15), (0, 128 - small.shape[1])))
    units, out_rows = gate_weight.shape[0], out_weight.shape[0]
    qkv_all, out_all, small_all = gather_weights(
        qkv_weight, jnp.pad(out_weight, ((0, 16 - out_rows), (0, 0))), small
    )
    w_qkv = qkv_all.reshape(2048, D)
    w_out = out_all.reshape(2048, D)
    small_all = small_all.reshape(128, 16, 128)[:, 0]
    b_qkv = small_all[:, :16].reshape(2048).astype(F32)
    gain_one = small_all[:, 16:28].reshape(D).astype(F32)
    gain_two = small_all[:, 28:40].reshape(D).astype(F32)
    feature = lax.broadcasted_iota(jnp.int32, (384, 512), 0)
    slot = lax.broadcasted_iota(jnp.int32, (384, 512), 1)
    spread = (slot == feature // out_rows * 16 + feature % out_rows).astype(BF)

    first_row = block_index * TOK
    my_pos = lax.dynamic_slice_in_dim(positions_of(documents), first_row, TOK, 0)
    cosine, sine = rope_tables(my_pos)
    sine = jnp.concatenate([-sine[:, : HD // 2], sine[:, HD // 2 :]], axis=1)
    first = first_row + jnp.arange(TOK, dtype=jnp.int32) - my_pos
    first = jnp.broadcast_to(jnp.tile(first, GROUP)[None], (8, GQ))

    factor_one = lax.rsqrt(jnp.mean(inputs * inputs, axis=-1, keepdims=True) + norm_eps)
    normed_one = (inputs * factor_one * gain_one).astype(BF)
    qkv = dot(normed_one, w_qkv, (1, 1)) + b_qkv
    pad = ((0, ROWS - units), (0, 0))
    kv, queries, attended, slots, lse, w_gate, w_up, w_down, cot_rows = attend(
        qkv,
        cosine,
        sine,
        first,
        spread,
        jnp.pad(gate_weight, pad),
        jnp.pad(up_weight, pad),
        jnp.pad(down_weight, pad),
        cot_low,
    )
    w_gate, w_up, w_down = (w.reshape(-1, D) for w in (w_gate, w_up, w_down))
    cot_rows = cot_rows.reshape(-1, D)
    middle = inputs + dot(slots, w_out, (1, 0))
    factor_two = lax.rsqrt(jnp.mean(middle * middle, axis=-1, keepdims=True) + norm_eps)
    normed_two = (middle * factor_two * gain_two).astype(BF)

    rows_two = gather_rows(normed_two).reshape(-1, D)
    gate = dot(rows_two, w_gate, (1, 1))
    upward = dot(rows_two, w_up, (1, 1))
    hidden_grad = dot(cot_rows, w_down, (1, 1))
    sigma = jax.nn.sigmoid(gate)
    hidden = (gate * sigma * upward).astype(BF)
    gate_grad = (hidden_grad * upward * sigma * (1.0 + gate * (1.0 - sigma))).astype(BF)
    upward_grad = (hidden_grad * gate * sigma).astype(BF)
    ffn_part = dot(hidden, w_down, (1, 0)).astype(BF)
    grad_part = (dot(gate_grad, w_gate, (1, 0)) + dot(upward_grad, w_up, (1, 0))).astype(BF)
    rows_lead = lead_of(ROW_DIMS) + (TOK, D)
    ffn_total, normed_two_grad = scatter_rows(
        ffn_part.reshape(rows_lead), grad_part.reshape(rows_lead)
    )
    layer_out = (middle + ffn_total).astype(BF)

    cot_full = cot_low.astype(F32)
    scaled_two = gain_two * normed_two_grad
    gain_two_grad = jnp.sum(normed_two_grad * middle * factor_two, axis=0)
    middle_grad = (
        cot_full
        + factor_two * scaled_two
        - middle * factor_two**3 * jnp.mean(scaled_two * middle, axis=-1, keepdims=True)
    )
    branch_grad = middle_grad.astype(BF)
    grad_slots = dot(branch_grad, w_out, (1, 1)).astype(BF)
    ffn_lead = lead_of(FFN_DIMS) + (ROWS, D)
    parts = tuple(
        dot(a, b, (0, 0)).astype(BF).reshape(ffn_lead)
        for a, b in ((gate_grad, rows_two), (upward_grad, rows_two), (hidden, cot_rows))
    )
    qkv_grad, *parts = attend_back(
        kv, queries, attended, grad_slots, lse, first, cosine, sine, spread, parts
    )
    normed_one_grad = dot(qkv_grad, w_qkv, (1, 0))
    scaled_one = gain_one * normed_one_grad
    gain_one_grad = jnp.sum(normed_one_grad * inputs * factor_one, axis=0)
    input_grad = (
        middle_grad
        + factor_one * scaled_one
        - inputs * factor_one**3 * jnp.mean(scaled_one * inputs, axis=-1, keepdims=True)
    )

    lead = lead_of(AXES)
    qkv_part = dot(qkv_grad, normed_one, (0, 0)).astype(BF)
    out_part = dot(slots, branch_grad, (0, 0)).astype(BF)
    bias_part = jnp.sum(qkv_grad.astype(F32), axis=0)
    small_part = jnp.concatenate(
        [
            bias_part.reshape(128, 16),
            gain_one_grad.reshape(128, 12),
            gain_two_grad.reshape(128, 12),
        ],
        axis=1,
    ).astype(BF)
    small_part = jnp.pad(small_part[:, None], ((0, 0), (0, 15), (0, 88)))
    qkv_sum, out_sum, small_sum, gate_sum, up_sum, down_sum = scatter_weight_grads(
        qkv_part.reshape(lead + (16, D)),
        out_part.reshape(lead + (16, D)),
        small_part.reshape(lead + (16, 128)),
        parts,
    )
    return (
        layer_out[None],
        input_grad[None],
        qkv_sum,
        small_sum[0, :16],
        out_sum[:out_rows],
        small_sum[0, 16:40].reshape(2, 12),
        gate_sum[:units],
        up_sum[:units],
        down_sum[:units],
    )


def solution(mesh):
    fine = Mesh(mesh.devices.reshape(tuple(SIZE[a] for a in AXES)), AXES)
    dp, ctx = ("zl", "c"), ("y", "x", "zh")
    in_specs = (
        P(dp, ctx, None),
        P(AXES, None),
        P(AXES),
        P(AXES, None),
        P(None, AXES),
        P(AXES, None),
        P(AXES, None),
        P(AXES, None),
        P(dp, None),
        P(dp, ctx, None),
    )
    out_specs = (
        P(dp, ctx, None),
        P(dp, ctx, None),
        P(AXES, None),
        P(AXES),
        P(AXES, None),
        P(None, AXES),
        P(AXES, None),
        P(AXES, None),
        P(AXES, None),
    )
    return jax.shard_map(local, mesh=fine, in_specs=in_specs, out_specs=out_specs, check_vma=False)
```

time: 788 us -> 537 us (0.68)
  Pallas kernels: 548 us -> 416 us
  local copies, waits for them, and re-layouts: 106 us -> 19.7 us
  other arithmetic: 29.9 us -> 8.7 us
  matrix products: 93.8 us -> 83 us
    pallas_call x4, Pallas kernels: 464 us -> 336 us  [the longest x1 117 us: attend(): pl.pallas_call(attend_kernel, out_shape=(jax.ShapeDtypeStruct(lead_of(KV_...]
    convert_element_type x8 -> x3, local copies, waits for them, and re-layouts: 24.7 us -> 0.28 us  [the longest x1 0.1 us: local(): gain_two = small_all[:, 28:40].reshape(D).astype(F32)]
    concatenate x7 -> x6, local copies, waits for them, and re-layouts: 24.4 us -> 0.53 us  [local(): jnp.concatenate([bias_part.reshape(128, 16), gain_one_grad.reshape(128, 1...]
    reshape x4 -> x1, local copies, waits for them, and re-layouts: 16.4 us -> 0.74 us  [local(): small = jnp.concatenate([qkv_bias, norm_gains.reshape(-1)])[None]]
    concatenate x6 -> x2, other arithmetic: 14 us -> 0.12 us  [the longest x1 0.09 us: local(): sine = jnp.concatenate([-sine[:, :HD // 2], sine[:, HD // 2:]], axis=1)]
    dot_general x7 -> x0, matrix products: 11.3 us -> none  [the longest x2 3.09 us: scores_of(): jnp.einsum('qkgd,skd->kgqs', queries, key_part, preferred_element_type=F32)]
    slice x8 -> x2, local copies, waits for them, and re-layouts: 9.8 us -> 1.76 us  [the longest x1 0.99 us: local(): small_all = small_all.reshape(128, 16, 128)[:, 0]]
where the time goes in v2:
time: 537 us; the launch traced here: 529 us
  Pallas kernels  416 us (77%)
  matrix products  83 us (15%)
  local copies, waits for them, and re-layouts  19.7 us (4%)
  other arithmetic  8.7 us (2%)
    pallas_call x1, Pallas kernels, attend(): pl.pallas_call(attend_kernel, out_shape=(jax.ShapeDtypeStruct(lead_of(KV_...  117 us
    pallas_call x1, Pallas kernels, attend_back(): pl.pallas_call(attend_back_kernel, out_shape=(jax.ShapeDtypeStruct((TOK,...  112 us
    dot_general x15, matrix products, dot(): lax.dot_general(a, b, ((dims[:1], dims[1:]), ((), ())), preferred_element...  83 us
    pallas_call x1, Pallas kernels, scatter_weight_grads(): pl.pallas_call(weight_grads_kernel, out_shape=(attn, attn, jax.ShapeDtype...  56.4 us
    pallas_call x1, Pallas kernels, gather_weights(): pl.pallas_call(weights_kernel, out_shape=(every, every, smalls), in_specs...  50.8 us
    pallas_call x1, Pallas kernels, scatter_rows(): pl.pallas_call(rows_scatter_kernel, out_shape=(one, one), in_specs=[ANY]...  44.1 us
    pallas_call x1, Pallas kernels, gather_rows(): pl.pallas_call(rows_kernel, out_shape=jax.ShapeDtypeStruct((4, 2, TOK, D)...  35.9 us

profile of v2, /device:TPU:0, one launch (start us, length us, event | category | flops | bytes accessed | tf_op | source)
XLA Modules:
  0.0 528.9 jit_solution(5923450358571609341)
XLA Ops:
  0.7 0.9 convert_reduce_fusion
  1.6 0.2 reduce-window.8
  1.8 0.7 reshape.235
  2.5 0.7 maximum_bitcast_fusion
  3.2 1.2 fusion.5
  4.4 0.6 pad.23.small
  5.0 0.8 select_reduce_fusion
  5.9 0.1 add_subtract_fusion
  6.0 1.4 pad.22.out
  7.4 0.1 broadcast_multiply_fusion
  7.5 0.3 fusion.27
  7.8 0.1 slice_negate_fusion
  7.9 0.1 pad_maximum_fusion.1.refs_2_.refs_7_
  8.0 1.0 pad.24.refs_5_
  9.0 1.0 pad.25.refs_6_
  10.0 1.0 pad.26.refs_7_
  10.9 0.5 fusion.16.refs_4_.refs_8_
  11.5 50.8 %shard_map.169 = (bf16[2,2,4,4,2,16,1536]{6,5,4,3,2,1,0:T(8,128)(2,1)}, bf16[2,2,4,4,2,16,1536]{6,5,4,3,2,1,0:T(8,128)(2,1)}, bf16[2,2,4,4,2,16,128]{6,5,4,3,2,1,0:T(8,128)(2,1)}) custom-call(bf16[16,1536]{1,0:T(8,128)(2,1)} %qkv.1, bf16[16,1536]{1,0:T(8,128)(2,1)} %pad.22.out, bf16[16,128]{1,0:T(8,128)(2,1)} %pad.23.small), custom_call_target="tpu_custom_call" | custom-call | tf_op jit(solution)/shard_map/pallas_call | solution.py:151
  62.2 1.0 slice.48
  63.3 0.1 reshape.256
  63.4 0.1 slice_convert_fusion
  63.5 0.1 reshape.257
  63.6 0.1 reshape.255
  63.7 5.1 convolution_add_fusion.1.refs_0_
  68.8 116.5 %shard_map.170 = (bf16[4,4,2,128,512]{4,3,2,1,0:T(8,128)(2,1)}, bf16[128,1536]{1,0:T(8,128)(2,1)S(1)}, f32[128,1536]{1,0:T(8,128)S(1)}, bf16[128,2048]{1,0:T(8,1...) custom-call(f32[128,2048]{1,0:T(8,128)S(1)} %convolution_add_fusion., ...), custom_call_target="tpu_custom_call" | custom-call | tf_op jit(solution)/shard_map/pallas_call | solution.py:293
  185.4 1.1 multiply_reduce_fusion.2
  186.5 0.9 multiply_convert_fusion.3.block
  187.4 35.9 %shard_map.171 = bf16[4,2,128,1536]{3,2,1,0:T(8,128)(2,1)} custom-call(bf16[128,1536]{1,0:T(8,128)(2,1)} %multiply_convert_fusion.3.block), custom_call_target="tpu_custom_call" | custom-call | tf_op jit(solution)/shard_map/pallas_call | solution.py:459
  223.3 7.5 %fusion.37 = f32[1024,1280]{1,0:T(8,128)S(1)} fusion(bf16[1024,1536]{1,0:T(8,128)(2,1)} %bitcast.111, bf16[1280,1536]{1,0:T(8,128)(2,1)} %bitcast.124), kind=kOutput, calls=%fused_computation.89 | convolution fusion | flops 4026531840 | bytes 12320768 | tf_op jit(solution)/shard_map/dot_general | solution.py:665
  230.8 6.1 %fusion.36 = f32[1024,1280]{1,0:T(8,128)} fusion(bf16[1024,1536]{1,0:T(8,128)(2,1)S(1)} %bitcast.113, bf16[1280,1536]{1,0:T(8,128)(2,1)S(1)} %bitcast.126), kind=kOutput, calls=%fused_computation.88 | convolution fusion | flops 4026531840 | bytes 12320768 | tf_op jit(solution)/shard_map/dot_general | solution.py:665
  237.0 9.9 %multiply_convert_fusion = (bf16[1024,1280]{1,0:T(8,128)(2,1)}, bf16[1024,1280]{1,0:T(8,128)(2,1)}, bf16[1024,1280]{1,0:T(8,128)(2,1)}) fusion(f32[1024,1280]{1,0:T(8,128)} %fusion.36, f32[1024,1280]{1,0:T(8,128)S(1)} %fusion.37, bf16[1024,1536]{1,0:T(8,128)(2,1)S(1)} %bitcast.130, bf16[1280,1536]{1,0:T(8,128)(2,1)S(1)} %bitcast.128), kind=kOutput, calls=%fused_computation.6 | convolution fusion | flops 4047503360 | bytes 25427968 | tf_op jit(solution)/shard_map/dot_general | solution.py:665
  246.9 6.3 %convolution_convert_fusion.5 = bf16[1024,1536]{1,0:T(8,128)(2,1)S(1)} fusion(bf16[1024,1280]{1,0:T(8,128)(2,1)} %get-tuple-element.69, bf16[1280,1536]{1,0:T(8,128)(2,1)S(1)} %bitcast.129), kind=kOutput, calls=%fused_computation.10 | convolution fusion | flops 4028104704 | bytes 9699328 | tf_op jit(solution)/shard_map/dot_general | solution.py:665
  253.2 6.0 %convolution_convert_fusion = bf16[1280,1536]{1,0:T(8,128)(2,1)} fusion(bf16[1024,1280]{1,0:T(8,128)(2,1)S(1)} %copy-done.20, bf16[1024,1536]{1,0:T(8,128)(2,1)S(1)} %bitcast.131), kind=kOutput, calls=%fused_computation | convolution fusion | flops 4028497920 | bytes 9699328 | tf_op jit(solution)/shard_map/dot_general | solution.py:665
  259.2 4.2 fusion.38
  263.4 5.7 %add_convert_fusion = bf16[1024,1536]{1,0:T(8,128)(2,1)} fusion(f32[1024,1536]{1,0:T(8,128)S(1)} %fusion.38, bf16[1024,1280]{1,0:T(8,128)(2,1)S(1)} %copy-done.17, bf16[1280,1536]{1,0:T(8,128)(2,1)S(1)} %bitcast.125), kind=kOutput, calls=%fused_computation.5 | convolution fusion | flops 4029677568 | bytes 15990784 | tf_op jit(solution)/shard_map/dot_general | solution.py:665
  269.1 44.1 %shard_map.172 = (f32[128,1536]{1,0:T(8,128)S(1)}, f32[128,1536]{1,0:T(8,128)S(1)}) custom-call(bf16[4,2,128,1536]{3,2,1,0:T(8,128)(2,1)S(1)} %bitcast.98, bf16[4,2,128,1536]{3,2,1,0:T(8,128)(2,1)} %bitcast.115), custom_call_target="tpu_custom_call" | custom-call | tf_op jit(solution)/shard_map/pallas_call | solution.py:563
  313.2 0.2 multiply_reduce_fusion
  313.4 1.1 multiply_subtract_fusion
  314.6 2.9 convolution_convert_fusion.6.refs_3_
  317.5 0.1 concatenate.31
  317.6 0.1 copy.29
  317.7 9.1 %convolution_convert_fusion.1 = bf16[1280,1536]{1,0:T(8,128)(2,1)} fusion(bf16[1024,1280]{1,0:T(8,128)(2,1)} %get-tuple-element.67, bf16[1024,1536]{1,0:T(8,128)(2,1)} %bitcast.112), kind=kOutput, calls=%fused_computation.1 | convolution fusion | flops 4028497920 | bytes 9699328 | tf_op jit(solution)/shard_map/dot_general | solution.py:665
  326.8 5.9 %convolution_convert_fusion.2 = bf16[1280,1536]{1,0:T(8,128)(2,1)} fusion(bf16[1024,1280]{1,0:T(8,128)(2,1)S(1)} %copy-done.19, bf16[1024,1536]{1,0:T(8,128)(2,1)S(1)} %bitcast.114), kind=kOutput, calls=%fused_computation.2 | convolution fusion | flops 4028497920 | bytes 9699328 | tf_op jit(solution)/shard_map/dot_general | solution.py:665
  332.7 112.3 %shard_map.173 = (bf16[128,2048]{1,0:T(8,128)(2,1)}, bf16[2,2,80,768]{3,2,1,0:T(8,128)(2,1)}, bf16[4,80,768]{2,1,0:T(8,128)(2,1)}, bf16[2,2,80,768]{3,2,1,0:T(8,...) custom-call(bf16[4,4,2,128,512]{4,3,2,1,0:T(8,128)(2,1)} %get-tuple-element.46., ...), custom_call_target="tpu_custom_call" | custom-call | tf_op jit(solution)/shard_map/pallas_call | solution.py:424
  445.0 4.2 fusion.13
  449.2 1.2 fusion.8
  450.4 0.1 reduce
  450.5 0.1 concatenate.29
  450.6 0.1 copy.27
  450.6 0.1 concatenate.30
  450.8 0.1 copy.28
  450.9 0.1 copy.32
  451.0 0.9 pad.27.clone
  451.9 4.5 convolution_convert_fusion.3
  456.4 4.6 convolution_convert_fusion.4
  461.0 56.4 %shard_map.174 = (f32[16,1536]{1,0:T(8,128)}, f32[16,1536]{1,0:T(8,128)}, f32[16,128]{1,0:T(8,128)}, f32[80,1536]{1,0:T(8,128)}, f32[80,1536]{1,0:T(8,128)}, /*index=5*/f32[80,1536]{1,0:T(8,128)}) custom-call(bf16[2,2,4,4,2,16,1536]{6,5,4,3,2,1,0:T(8,128)(2,1)} %bitcast.100, bf16[2,2,4,4,2,16,1536]{6,5,4,3,2,1,0:T(8,128)(2,1)} %bitcast.101, ...), custom_call_target="tpu_custom_call" | custom-call | tf_op jit(solution)/shard_map/pallas_call | solution.py:630
  517.4 0.8 slice_reduce_fusion
  518.1 1.2 slice_bitcast_fusion
  519.3 0.6 reshape_squeeze.3
  520.0 1.8 slice.45
  521.8 1.8 slice.46
  523.6 1.8 slice.47
  525.4 1.5 copy.37
  526.9 1.5 copy.38
  (61 shorter events, 0.2 us)
Async XLA Ops:
  0.6 63.0 %copy-start.9 = (bf16[1,128,1536]{2,1,0:T(8,128)(2,1)S(1)}, bf16[1,128,1536]{2,1,0:T(8,128)(2,1)}, u32[]{:S(2)}) copy-start(bf16[1,128,1536]{2,1,0:T(8,128)(2,1)} %param.10) | copy-start | bytes 1179652
  6.0 62.8 %copy-start.6 = (s32[8,768]{1,0:T(8,128)}, s32[8,768]{1,0:T(8,128)S(1)}, u32[]{:S(2)}) copy-start(s32[8,768]{1,0:T(8,128)S(1)} %broadcast_in_dim.26.refs_3_.refs_5_) | copy-start | bytes 73732
  7.8 61.0 %copy-start.3 = (f32[128,128]{1,0:T(8,128)}, f32[128,128]{1,0:T(8,128)S(1)}, u32[]{:S(2)}) copy-start(f32[128,128]{1,0:T(8,128)S(1)} %get-tuple-element.75.refs_1_.refs_6_) | copy-start | bytes 196612
  8.0 60.8 %copy-start.4 = (f32[128,128]{1,0:T(8,128)}, f32[128,128]{1,0:T(8,128)S(1)}, u32[]{:S(2)}) copy-start(f32[128,128]{1,0:T(8,128)S(1)} %pad_maximum_fusion.1.refs_2_.refs_7_) | copy-start | bytes 196612
  11.5 57.4 %copy-start = (bf16[384,512]{1,0:T(8,128)(2,1)}, bf16[384,512]{1,0:T(8,128)(2,1)S(1)}, u32[]{:S(2)}) copy-start(bf16[384,512]{1,0:T(8,128)(2,1)S(1)} %fusion.16.refs_4_.refs_8_) | copy-start | bytes 1179652
  63.4 5.4 %copy-start.1 = (bf16[1,128,1536]{2,1,0:T(8,128)(2,1)S(1)}, bf16[1,128,1536]{2,1,0:T(8,128)(2,1)}, u32[]{:S(2)}) copy-start(bf16[1,128,1536]{2,1,0:T(8,128)(2,1)} %param.19) | copy-start | bytes 1179652
  63.7 121.7 %copy-start.8 = (bf16[2,2,4,4,2,16,1536]{6,5,4,3,2,1,0:T(8,128)(2,1)S(1)}, bf16[2,2,4,4,2,16,1536]{6,5,4,3,2,1,0:T(8,128)(2,1)}, u32[]{:S(2)}) copy-start(bf16[2,2,4,4,2,16,1536]{6,5,4,3,2,1,0:T(8,128)(2,1)} %get-tuple-element.39) | copy-start | bytes 18874372
  185.4 1.1 copy-start.2
  185.4 1.1 copy-start.5
  185.4 1.1 copy-start.7
  223.3 7.5 %copy-start.11 = (bf16[4,2,128,1536]{3,2,1,0:T(8,128)(2,1)S(1)}, bf16[4,2,128,1536]{3,2,1,0:T(8,128)(2,1)}, u32[]{:S(2)}) copy-start(bf16[4,2,128,1536]{3,2,1,0:T(8,128)(2,1)} %shard_map.171) | copy-start | bytes 9437188
  223.3 7.5 %copy-start.14 = (bf16[2,4,2,80,1536]{4,3,2,1,0:T(8,128)(2,1)S(1)}, bf16[2,4,2,80,1536]{4,3,2,1,0:T(8,128)(2,1)}, u32[]{:S(2)}) copy-start(bf16[2,4,2,80,1536]{4,3,2,1,0:T(8,128)(2,1)} %get-tuple-element.40) | copy-start | bytes 11796484
  230.8 6.1 %copy-start.15 = (bf16[2,4,2,80,1536]{4,3,2,1,0:T(8,128)(2,1)S(1)}, bf16[2,4,2,80,1536]{4,3,2,1,0:T(8,128)(2,1)}, u32[]{:S(2)}) copy-start(bf16[2,4,2,80,1536]{4,3,2,1,0:T(8,128)(2,1)} %get-tuple-element.42) | copy-start | bytes 11796484
  230.8 6.1 %copy-start.16 = (bf16[4,2,128,1536]{3,2,1,0:T(8,128)(2,1)S(1)}, bf16[4,2,128,1536]{3,2,1,0:T(8,128)(2,1)}, u32[]{:S(2)}) copy-start(bf16[4,2,128,1536]{3,2,1,0:T(8,128)(2,1)} %get-tuple-element.43) | copy-start | bytes 9437188
  246.9 6.3 %copy-start.20 = (bf16[1024,1280]{1,0:T(8,128)(2,1)S(1)}, bf16[1024,1280]{1,0:T(8,128)(2,1)}, u32[]{:S(2)}) copy-start(bf16[1024,1280]{1,0:T(8,128)(2,1)} %get-tuple-element.69) | copy-start | bytes 7864324
  253.2 6.0 %copy-start.18 = (bf16[1024,1280]{1,0:T(8,128)(2,1)S(1)}, bf16[1024,1280]{1,0:T(8,128)(2,1)}, u32[]{:S(2)}) copy-start(bf16[1024,1280]{1,0:T(8,128)(2,1)} %get-tuple-element.68) | copy-start | bytes 7864324
  259.2 4.2 copy-start.13
  259.2 4.2 copy-start.17
  269.1 45.5 %slice-start = ((s8[6291456]{0:T(1024)(128)(4,1)}), s8[4194304]{0:T(1024)(128)(4,1)S(1)}, s32[]{:S(2)}) async-start(s8[6291456]{0:T(1024)(128)(4,1)} %bitcast.105), calls=%async_computation | async-start | bytes 8388608
  269.1 45.5 %slice-start.1 = ((s8[6291456]{0:T(1024)(128)(4,1)}), s8[2097152]{0:T(1024)(128)(4,1)S(1)}, s32[]{:S(2)}) async-start(s8[6291456]{0:T(1024)(128)(4,1)} %bitcast.105), calls=%async_computation.1 | async-start | bytes 4194304
  317.7 9.1 %copy-start.12 = (bf16[4,2,128,1536]{3,2,1,0:T(8,128)(2,1)S(1)}, bf16[4,2,128,1536]{3,2,1,0:T(8,128)(2,1)}, u32[]{:S(2)}) copy-start(bf16[4,2,128,1536]{3,2,1,0:T(8,128)(2,1)} %shard_map.171) | copy-start | bytes 9437188
  317.7 9.1 %copy-start.19 = (bf16[1024,1280]{1,0:T(8,128)(2,1)S(1)}, bf16[1024,1280]{1,0:T(8,128)(2,1)}, u32[]{:S(2)}) copy-start(bf16[1024,1280]{1,0:T(8,128)(2,1)} %get-tuple-element.68) | copy-start | bytes 7864324
  445.0 5.4 %copy-start.10 = (bf16[128,2048]{1,0:T(8,128)(2,1)S(1)}, bf16[128,2048]{1,0:T(8,128)(2,1)}, u32[]{:S(2)}) copy-start(bf16[128,2048]{1,0:T(8,128)(2,1)} %get-tuple-element.50) | copy-start | bytes 1572868

commit v3 on v2

v3 whole, which is shorter than its diff:
```python
import math

import jax
import jax.numpy as jnp
from jax import lax
from jax.experimental import pallas as pl
from jax.experimental.pallas import tpu as pltpu
from jax.sharding import Mesh
from jax.sharding import PartitionSpec as P

H = 12
KVH = 2
HD = 128
HQ = 1536
D = 1536
TOK = 128
ROWS = 80

norm_eps = 1e-06
rope_base = 1000000.0
doc_kinds = 3

AXES = ("zl", "c", "y", "x", "zh")
SIZE = {"zl": 2, "c": 2, "y": 4, "x": 4, "zh": 2}
PARTS_OF = {"z": ("zl", "zh"), "x": ("x",), "y": ("y",), "c": ("c",), "zh": ("zh",)}
REACH = {"z": (1, 2, 3), "x": (1, 2, 3), "y": (1, 2, 3), "c": (1,), "zh": (1,)}
BF = jnp.bfloat16
F32 = jnp.float32
ANY = pl.BlockSpec(memory_space=pl.ANY)
VMEM = pl.BlockSpec(memory_space=pltpu.VMEM)


def here():
    return {a: lax.axis_index(a) for a in AXES}


def peer(me, axis, k):
    to = dict(me)
    if axis == "z":
        z = lax.rem(me["zh"] * 2 + me["zl"] + k, 4)
        to["zl"], to["zh"] = lax.rem(z, 2), lax.div(z, 2)
    else:
        to[axis] = lax.rem(me[axis] + k, SIZE[axis])
    return to


def device_id(at):
    return tuple(at[a] for a in AXES)


def place(dims, at, whole, tail=()):
    return tuple(slice(None) if d in whole else at[d] for d in dims) + tuple(tail)


class Links:
    def __init__(self, me, send, recv):
        self.me, self.send, self.recv, self.used = me, send, recv, 0

    def copy(self, src, dst, axis, k):
        i = self.used
        self.used += 1
        c = pltpu.make_async_remote_copy(
            src_ref=src,
            dst_ref=dst,
            send_sem=self.send.at[i],
            recv_sem=self.recv.at[i],
            device_id=device_id(peer(self.me, axis, k)),
            device_id_type=pl.DeviceIdType.MESH,
        )
        c.start()
        return c


def greet(me, axes):
    barrier = pltpu.get_barrier_semaphore()
    count = 0
    for axis in axes:
        for k in REACH[axis]:
            pl.semaphore_signal(
                barrier,
                inc=1,
                device_id=device_id(peer(me, axis, k)),
                device_id_type=pl.DeviceIdType.MESH,
            )
            count += 1
    pl.semaphore_wait(barrier, count)


def halves_of(tail, cols):
    rows = tail[:-1] if tail else (slice(None),)
    start = tail[-1].start if tail else 0
    cut = cols // 2
    return tuple(rows + (slice(start + cut * i, start + cut * (i + 1)),) for i in range(2))


def gather_stream(links, block, buf, dims, tail, order):
    me = links.me
    whole = ()
    cols = block.shape[-1]
    for n, axis in enumerate(order):
        mine = place(dims, me, whole, tail)
        src = block if n == 0 else buf.at[mine]
        near = (1, 3) if len(REACH[axis]) == 3 else (1,)
        copies = [links.copy(src, buf.at[mine], axis, k) for k in near]
        yield
        for c in copies:
            c.wait()
        if len(near) == 2:
            copies = []
            for k, half in zip(near, halves_of(tail, cols), strict=True):
                theirs = buf.at[place(dims, peer(me, axis, 4 - k), whole, half)]
                copies.append(links.copy(theirs, theirs, axis, k))
            yield
            for c in copies:
                c.wait()
        whole = whole + PARTS_OF[axis]


def run_streams(streams):
    live = list(streams)
    while live:
        live = [s for s in live if next(s, live) is not live]


def step(streams):
    for s in streams:
        next(s, None)


def count_gather(orders):
    return sum((1, 4)[len(REACH[a]) // 3] for order in orders for a in order)


def count_scatter(orders):
    return sum(len(REACH[a]) for order in orders for a in order)


THIRDS = tuple((slice(None), slice(512 * i, 512 * (i + 1))) for i in range(3))
ORDERS = (("x", "y", "z"), ("y", "z", "x"), ("z", "x", "y"))
HALVES = tuple((slice(None), slice(768 * i, 768 * (i + 1))) for i in range(2))
FFN_ORDERS = (("y", "z"), ("z", "y"))
FFN_DIMS = ("zl", "y", "zh")
ROW_DIMS = ("x", "c")
KV_DIMS = ("y", "x", "zh")


def weights_kernel(qkv, out, small, qkv_all, out_all, small_all, send, recv, local):
    me = here()
    links = Links(me, send, recv)
    own = []
    pairs = ((qkv, qkv_all), (out, out_all), (small, small_all))
    for i, (a, b) in enumerate(pairs):
        own.append(pltpu.make_async_copy(a, b.at[place(AXES, me, ())], local.at[i]))
        own[-1].start()
    greet(me, ("x", "y", "z", "c"))
    for c in own:
        c.wait()
    streams = []
    for block, buf in pairs[:2]:
        for order, tail in zip(ORDERS, THIRDS, strict=True):
            streams.append(
                gather_stream(links, block.at[tail], buf, AXES, tail, order + ("c",))
            )
    streams.append(gather_stream(links, small, small_all, AXES, (), ORDERS[0] + ("c",)))
    run_streams(streams)


def gather_weights(qkv, out, small):
    every = jax.ShapeDtypeStruct(lead_of(AXES) + (16, D), BF)
    smalls = jax.ShapeDtypeStruct(lead_of(AXES) + (16, 256), BF)
    copies = 2 * count_gather([o + ("c",) for o in ORDERS]) + count_gather([ORDERS[0] + ("c",)])
    return pl.pallas_call(
        weights_kernel,
        out_shape=(every, every, smalls),
        in_specs=[ANY] * 3,
        out_specs=(ANY,) * 3,
        scratch_shapes=[
            pltpu.SemaphoreType.DMA((copies,)),
            pltpu.SemaphoreType.DMA((copies,)),
            pltpu.SemaphoreType.DMA((3,)),
        ],
        compiler_params=pltpu.CompilerParams(collective_id=1, has_side_effects=True),
    )(qkv, out, small)


def lead_of(dims):
    return tuple(SIZE[d] for d in dims)


def rest_of(dims, axis):
    return tuple(d for d in dims if d not in PARTS_OF[axis])


def scatter_scratch(dims, order, rows, cols):
    shapes = []
    for axis in order:
        dims = rest_of(dims, axis)
        shapes.append(pltpu.VMEM((len(REACH[axis]),) + lead_of(dims) + (rows, cols), BF))
        shapes.append(pltpu.VMEM(lead_of(dims) + (rows, cols), BF))
    return shapes


def sum_blocks(own, arrived, out, lead, rows, step):
    count = 1
    for n in lead:
        count *= n
    per = rows // step
    parts = arrived.shape[0]

    def body(i, carry):
        block, row = lax.div(i, per), lax.rem(i, per)
        index = []
        for n in reversed(lead):
            index.append(lax.rem(block, n))
            block = lax.div(block, n)
        at = tuple(reversed(index)) + (pl.ds(pl.multiple_of(row * step, step), step),)
        total = own[at].astype(F32)
        for p in range(parts):
            total = total + arrived[(p,) + at].astype(F32)
        out[at] = total.astype(out.dtype)
        return carry

    lax.fori_loop(0, count * per, body, 0)


def scatter_stream(links, local, source, dims, tail, order, scratch, out, rows, step):
    me = links.me
    now = None
    for n, axis in enumerate(order):
        arrived, own = scratch[2 * n], scratch[2 * n + 1]
        gone = PARTS_OF[axis]
        keep = tuple(d for d in dims if d not in gone)
        end = tail if n == 0 else ()
        base = source if n == 0 else now
        copies = []
        for k in REACH[axis]:
            to = peer(me, axis, k)
            src = base.at[place(dims, to, keep, end)]
            copies.append(links.copy(src, arrived.at[k - 1], axis, k))
        held = base.at[place(dims, me, keep, end)]
        staged = n == 0 and local is not None
        if staged:
            mine = pltpu.make_async_copy(held, own, local)
            mine.start()
        yield
        if staged:
            mine.wait()
            held = own
        for c in copies:
            c.wait()
        target = out if n == len(order) - 1 else own
        sum_blocks(held, arrived, target, lead_of(keep), rows, step)
        now, dims = own, keep


FIRST_STAGE = (("y",), ("z",))
LAST_STAGE = (("z",), ("y",))
KV_ORDERS = (("y", "x", "zh"), ("x", "y", "zh"))
ALL_ORDERS = tuple(("c",) + o for o in ORDERS)


def first_stage_scratch():
    scratch, sums = [], []
    for order in FIRST_STAGE:
        scratch += scatter_scratch(FFN_DIMS, order, ROWS, 768)
        sums.append(jax.ShapeDtypeStruct(lead_of(rest_of(FFN_DIMS, order[0])) + (ROWS, 768), BF))
    return scratch, sums


def first_stage(links, local, used, part, sums, scratch):
    return [
        scatter_stream(
            links,
            local.at[used + i],
            part,
            FFN_DIMS,
            HALVES[i],
            FIRST_STAGE[i],
            scratch[2 * i : 2 * i + 2],
            sums[i],
            ROWS,
            16,
        )
        for i in range(2)
    ]


def rows_scatter_kernel(rows, part, out, sum_a, sum_b, send, recv, local, *scratch):
    me = here()
    links = Links(me, send, recv)
    greet(me, ("x", "y", "z", "c"))
    streams = [
        scatter_stream(links, local.at[2], rows, ROW_DIMS, (), ("c", "x"), scratch[4:], out, TOK, 16)
    ]
    weights = first_stage(links, local, 0, part, (sum_a, sum_b), scratch[:4])
    step(streams)
    step(weights)
    run_streams(streams)
    step(weights)


def scatter_rows(rows, part):
    copies = count_scatter([("c", "x")]) + count_scatter(FIRST_STAGE)
    scratch, sums = first_stage_scratch()
    return pl.pallas_call(
        rows_scatter_kernel,
        out_shape=(jax.ShapeDtypeStruct((TOK, D), F32),) + tuple(sums),
        in_specs=[ANY] * 2,
        out_specs=(VMEM,) * 3,
        scratch_shapes=[
            pltpu.SemaphoreType.DMA((copies,)),
            pltpu.SemaphoreType.DMA((copies,)),
            pltpu.SemaphoreType.DMA((3,)),
        ]
        + scratch
        + scatter_scratch(ROW_DIMS, ("c", "x"), TOK, D),
        compiler_params=pltpu.CompilerParams(
            collective_id=4, has_side_effects=True, vmem_limit_bytes=48 * 2**20
        ),
    )(rows, part)


GROUP = H // KVH
GQ = GROUP * TOK
KEYS = 512
SCALE = HD**-0.5
TO_LOG2 = SCALE * math.log2(math.e)


def head(h):
    return slice(128 * h, 128 * (h + 1))


def turned(v):
    return pltpu.roll(v, 64, 1)


def key_blocks():
    ctx = lax.axis_index("y") * 8 + lax.axis_index("x") * 2 + lax.axis_index("zh")
    return lax.div(ctx, 4) + 1, ctx * TOK


def key_block_of(ref, b, cols):
    return ref[lax.div(b, 2), pl.ds(lax.rem(b, 2) * 2, 2), :, :, cols].reshape(KEYS, HD)


def allowed_keys(b, first, row):
    key = b * KEYS + lax.broadcasted_iota(jnp.int32, (KEYS, GQ), 0)
    query = row + lax.rem(lax.broadcasted_iota(jnp.int32, (1, GQ), 1), TOK)
    return (key <= query) & (key >= first)


def mm(a, b, contract):
    return lax.dot_general(
        a, b, ((contract[:1], contract[1:]), ((), ())), preferred_element_type=F32
    )


def attend_group(g, kv, qs, first, row, blocks, acc, stats):
    acc[...] = jnp.zeros_like(acc)
    stats[0:1] = jnp.full((1, GQ), -1e30, F32)
    stats[1:2] = jnp.zeros((1, GQ), F32)

    def body(b, carry):
        keys = key_block_of(kv, b, head(g))
        values = key_block_of(kv, b, head(2 + g))
        raw = mm(keys, qs[g], (1, 1)) * TO_LOG2
        raw = jnp.where(allowed_keys(b, first, row), raw, -1e30)
        old = stats[0:1]
        top = jnp.maximum(old, jnp.max(raw, axis=0, keepdims=True))
        probs = jnp.exp2(raw - top)
        shrink = jnp.exp2(old - top)
        stats[0:1] = top
        stats[1:2] = stats[1:2] * shrink + jnp.sum(probs, axis=0, keepdims=True)
        acc[...] = acc[...] * shrink + mm(values.T, probs.astype(BF), (1, 0))
        return carry

    lax.fori_loop(0, blocks, body, 0)


def attend_kernel(*refs):
    qkv, cosine, sine, first_ref, spread, tokens, gain = refs[:7]
    gate, up, down, cot, w_out_hbm = refs[7:12]
    kv, queries, attended, slots, lse, middle = refs[12:18]
    gate_all, up_all, down_all, cot_all, rows_all = refs[18:23]
    block, qs, acc, stats, w_out, normed, send, recv, local = refs[23:]
    me = here()
    links = Links(me, send, recv)
    own = []
    pairs = (
        (gate, gate_all, FFN_DIMS),
        (up, up_all, FFN_DIMS),
        (down, down_all, FFN_DIMS),
        (cot, cot_all, ROW_DIMS),
    )
    for i, (a, b, dims) in enumerate(pairs):
        own.append(pltpu.make_async_copy(a, b.at[place(dims, me, ())], local.at[i]))
        own[-1].start()
    cos, sin = cosine[...], sine[...]
    for g in range(KVH):
        part = qkv[:, head(H + g)]
        block[:, head(g)] = (part * cos + turned(part) * sin).astype(BF)
        block[:, head(2 + g)] = qkv[:, head(H + 2 + g)].astype(BF)
    own.append(pltpu.make_async_copy(block, kv.at[place(KV_DIMS, me, ())], local.at[4]))
    own[-1].start()
    fetch = pltpu.make_async_copy(w_out_hbm, w_out, local.at[5])
    fetch.start()
    greet(me, ("zh", "x", "y", "z", "c"))
    keys = []
    for half, order in enumerate((("zh", "x", "y"), ("zh", "y", "x"))):
        tail = (slice(None), slice(256 * half, 256 * (half + 1)))
        keys.append(gather_stream(links, block.at[tail], kv, KV_DIMS, tail, order))
    weights = []
    for a, b, _ in pairs[:3]:
        for order, tail in zip(FFN_ORDERS, HALVES, strict=True):
            weights.append(gather_stream(links, a.at[tail], b, FFN_DIMS, tail, order))
    cots = [gather_stream(links, cot, cot_all, ROW_DIMS, (), ("x", "c"))]
    step(keys)
    step(weights)
    for c in own:
        c.wait()
    step(keys)
    for h in range(H):
        part = qkv[:, head(h)]
        turned_q = (part * cos + turned(part) * sin).astype(BF)
        queries[:, head(h)] = turned_q
        qs[h // GROUP, (h % GROUP) * TOK : (h % GROUP + 1) * TOK, :] = turned_q
    step(keys)
    step(weights)
    step(keys)
    step(weights)
    step(keys)
    step(cots)
    step(keys)
    blocks, row = key_blocks()
    first = first_ref[0:1]
    for g in range(KVH):
        attend_group(g, kv, qs, first, row, blocks, acc, stats)
        total = stats[1:2]
        lse[g] = jnp.broadcast_to(stats[0:1] + jnp.log2(total), (8, GQ))
        acc[...] = acc[...] / total
        for i in range(GROUP):
            attended[:, head(GROUP * g + i)] = acc[:, head(i)].T
        step(cots)
    for i in range(4):
        part = attended[:, 384 * i : 384 * (i + 1)].astype(BF)
        slots[:, 512 * i : 512 * (i + 1)] = mm(part, spread[...], (1, 0)).astype(BF)
    fetch.wait()
    square = jnp.zeros((TOK, 1), F32)
    for i in range(3):
        cols = slice(512 * i, 512 * (i + 1))
        part = tokens[:, cols].astype(F32) + mm(slots[...], w_out[:, cols], (1, 0))
        middle[:, cols] = part
        square = square + jnp.sum(part * part, axis=1, keepdims=True)
    factor = lax.rsqrt(square / D + norm_eps)
    normed[...] = (middle[...] * factor * gain[0:1]).astype(BF)
    keep = pltpu.make_async_copy(normed, rows_all.at[place(ROW_DIMS, me, ())], local.at[6])
    keep.start()
    rows = [gather_stream(links, normed, rows_all, ROW_DIMS, (), ("x", "c"))]
    step(rows)
    step(weights)
    step(cots)
    step(rows)
    keep.wait()
    step(rows)
    step(rows)
    step(weights)


def attend(qkv, cosine, sine, first, spread, tokens, gain, gate, up, down, cot, w_out):
    ffn = jax.ShapeDtypeStruct(lead_of(FFN_DIMS) + (ROWS, D), BF)
    rows = jax.ShapeDtypeStruct(lead_of(ROW_DIMS) + (TOK, D), BF)
    copies = count_gather([("zh", "x", "y"), ("zh", "y", "x"), ("x", "c"), ("x", "c")])
    copies += 3 * count_gather(FFN_ORDERS)
    return pl.pallas_call(
        attend_kernel,
        out_shape=(
            jax.ShapeDtypeStruct(lead_of(KV_DIMS) + (TOK, 512), BF),
            jax.ShapeDtypeStruct((TOK, HQ), BF),
            jax.ShapeDtypeStruct((TOK, HQ), F32),
            jax.ShapeDtypeStruct((TOK, 2048), BF),
            jax.ShapeDtypeStruct((KVH, 8, GQ), F32),
            jax.ShapeDtypeStruct((TOK, D), F32),
            ffn,
            ffn,
            ffn,
            rows,
            rows,
        ),
        in_specs=[VMEM] * 7 + [ANY] * 5,
        out_specs=(VMEM,) * 6 + (ANY,) * 5,
        scratch_shapes=[
            pltpu.VMEM((TOK, 512), BF),
            pltpu.VMEM((KVH, GQ, HD), BF),
            pltpu.VMEM((HD, GQ), F32),
            pltpu.VMEM((8, GQ), F32),
            pltpu.VMEM((2048, D), BF),
            pltpu.VMEM((TOK, D), BF),
            pltpu.SemaphoreType.DMA((copies,)),
            pltpu.SemaphoreType.DMA((copies,)),
            pltpu.SemaphoreType.DMA((7,)),
        ],
        compiler_params=pltpu.CompilerParams(
            collective_id=2, has_side_effects=True, vmem_limit_bytes=48 * 2**20
        ),
    )(qkv, cosine, sine, first, spread, tokens, gain, gate, up, down, cot, w_out)


def grad_group(g, kv, qs, gs, lse, delta, first, row, blocks, query_grad, kv_grad):
    query_grad[...] = jnp.zeros_like(query_grad)

    def body(b, carry):
        at = (lax.div(b, 2), pl.ds(lax.rem(b, 2) * 2, 2), slice(None), slice(None))
        keys = key_block_of(kv, b, head(g))
        values = key_block_of(kv, b, head(2 + g))
        raw = mm(keys, qs[g], (1, 1)) * TO_LOG2
        probs = jnp.where(allowed_keys(b, first, row), jnp.exp2(raw - lse), 0.0)
        prob_grad = mm(values, gs[g], (1, 1))
        score_grad = (probs * (prob_grad - delta)).astype(BF)
        key_term = mm(score_grad, qs[g], (1, 0)) * SCALE
        value_term = mm(probs.astype(BF), gs[g], (1, 0))
        kv_grad[at + (head(g),)] = key_term.astype(BF).reshape(2, 2, TOK, HD)
        kv_grad[at + (head(2 + g),)] = value_term.astype(BF).reshape(2, 2, TOK, HD)
        query_grad[...] += mm(keys.T, score_grad, (1, 0))
        return carry

    lax.fori_loop(0, blocks, body, 0)


def attend_back_kernel(*refs):
    kv, queries, attended, grad_slots, lse, first_ref, cosine, sine, spread = refs[:9]
    gate_part, up_part, out_part, ffn_rows = refs[9:13]
    qkv_grad = refs[13]
    sums = refs[14:18]
    out_grad, ffn_total = refs[18:20]
    qs, gs, delta, query_grad, kv_grad, kv_out, send, recv, local = refs[20:29]
    scratch = list(refs[29:])

    def take(n):
        return [scratch.pop(0) for _ in range(n)]

    me = here()
    links = Links(me, send, recv)
    greet(me, ("zh", "x", "y", "z", "c"))
    weights = first_stage(links, local, 0, gate_part, sums[:2], take(4))
    weights += first_stage(links, local, 2, up_part, sums[2:], take(4))
    outs = []
    for i in range(3):
        outs.append(
            scatter_stream(
                links, local.at[4 + i], out_part, AXES, THIRDS[i], ALL_ORDERS[i], take(8), out_grad.at[THIRDS[i]], 16, 16
            )
        )
    rows = [
        scatter_stream(
            links, local.at[7], ffn_rows, ROW_DIMS, (), ("c", "x"), take(4), ffn_total, TOK, 16
        )
    ]
    step(weights)
    step(rows)
    step(outs)
    blocks, row = key_blocks()
    first = first_ref[0:1]
    for i in range(4):
        part = mm(grad_slots[:, 512 * i : 512 * (i + 1)], spread[...], (1, 1))
        for j in range(3):
            h = 3 * i + j
            one = part[:, head(j)]
            gs[h // GROUP, (h % GROUP) * TOK : (h % GROUP + 1) * TOK, :] = one.astype(BF)
            both = (one * attended[:, head(h)]).T
            delta[h // GROUP : h // GROUP + 1, head(h % GROUP)] = jnp.sum(
                both, axis=0, keepdims=True
            )
            qs[h // GROUP, (h % GROUP) * TOK : (h % GROUP + 1) * TOK, :] = queries[:, head(h)]

    def clear(b, carry):
        at = (lax.div(b, 2), pl.ds(lax.rem(b, 2) * 2, 2))
        kv_grad[at] = jnp.zeros((2, 2, TOK, 512), BF)
        return carry

    lax.fori_loop(blocks, 8, clear, 0)
    cos, sin = cosine[...], sine[...]
    for g in range(KVH):
        grad_group(
            g, kv, qs, gs, lse[g, 0:1], delta[g : g + 1], first, row, blocks, query_grad, kv_grad
        )
        for i in range(GROUP):
            one = query_grad[:, head(i)].T * SCALE
            qkv_grad[:, head(GROUP * g + i)] = (one * cos - turned(one) * sin).astype(BF)
    keys = []
    for half, order in enumerate(KV_ORDERS):
        tail = (slice(None), slice(256 * half, 256 * (half + 1)))
        keys.append(
            scatter_stream(
                links, None, kv_grad, KV_DIMS, tail, order, take(6), kv_out.at[half], TOK, 32
            )
        )
    step(keys)
    step(outs)
    step(rows)
    step(keys)
    step(outs)
    step(keys)
    step(outs)
    step(keys)
    for g in range(KVH):
        one = kv_out[0, :, head(g)]
        qkv_grad[:, head(H + g)] = (one * cos - turned(one) * sin).astype(BF)
        qkv_grad[:, head(H + 2 + g)] = kv_out[1, :, head(g)].astype(BF)
    step(rows)
    step(outs)
    step(weights)


def attend_back(
    kv, queries, attended, grad_slots, lse, first, cosine, sine, spread, gate_part, up_part, out_part, ffn_rows
):
    copies = count_scatter(KV_ORDERS) + 2 * count_scatter(FIRST_STAGE)
    copies += count_scatter(ALL_ORDERS) + count_scatter([("c", "x")])
    scratch, sums = [], []
    for _ in range(2):
        more, results = first_stage_scratch()
        scratch += more
        sums += results
    for order in ALL_ORDERS:
        scratch += scatter_scratch(AXES, order, 16, 512)
    scratch += scatter_scratch(ROW_DIMS, ("c", "x"), TOK, D)
    for order in KV_ORDERS:
        scratch += scatter_scratch(KV_DIMS, order, TOK, 256)
    return pl.pallas_call(
        attend_back_kernel,
        out_shape=(
            jax.ShapeDtypeStruct((TOK, 2048), BF),
            *sums,
            jax.ShapeDtypeStruct((16, D), F32),
            jax.ShapeDtypeStruct((TOK, D), F32),
        ),
        in_specs=[VMEM] * 9 + [ANY] * 4,
        out_specs=(VMEM,) * 7,
        scratch_shapes=[
            pltpu.VMEM((KVH, GQ, HD), BF),
            pltpu.VMEM((KVH, GQ, HD), BF),
            pltpu.VMEM((8, GQ), F32),
            pltpu.VMEM((HD, GQ), F32),
            pltpu.VMEM(lead_of(KV_DIMS) + (TOK, 512), BF),
            pltpu.VMEM((2, TOK, 256), F32),
            pltpu.SemaphoreType.DMA((copies,)),
            pltpu.SemaphoreType.DMA((copies,)),
            pltpu.SemaphoreType.DMA((8,)),
        ]
        + scratch,
        compiler_params=pltpu.CompilerParams(
            collective_id=5, has_side_effects=True, vmem_limit_bytes=60 * 2**20
        ),
    )(kv, queries, attended, grad_slots, lse, first, cosine, sine, spread, gate_part, up_part, out_part, ffn_rows)


def weight_grads_kernel(*refs):
    qkv, small = refs[:2]
    parts = refs[2:8]
    qkv_out, small_out = refs[8:10]
    ffn_outs = refs[10:13]
    send, recv, local = refs[13:16]
    scratch = list(refs[16:])
    me = here()
    links = Links(me, send, recv)
    greet(me, ("x", "y", "z", "c"))
    streams = []

    def add(source, dims, order, tail, target, rows):
        n = 2 * len(order)
        part = [scratch.pop(0) for _ in range(n)]
        streams.append(
            scatter_stream(
                links, local.at[len(streams)], source, dims, tail, order, part, target, rows, 16
            )
        )

    for order, tail in zip(ALL_ORDERS, THIRDS, strict=True):
        add(qkv, AXES, order, tail, qkv_out.at[tail], 16)
    add(small, AXES, ALL_ORDERS[0], (), small_out, 16)
    for i, source in enumerate(parts):
        order = LAST_STAGE[i % 2]
        dims = rest_of(FFN_DIMS, FIRST_STAGE[i % 2][0])
        add(source, dims, order, (), ffn_outs[i // 2].at[HALVES[i % 2]], ROWS)
    run_streams(streams)


def scatter_weight_grads(qkv, small, parts):
    copies = count_scatter(ALL_ORDERS) + count_scatter(ALL_ORDERS[:1])
    copies += 3 * count_scatter(LAST_STAGE)
    scratch = []
    for order in ALL_ORDERS:
        scratch += scatter_scratch(AXES, order, 16, 512)
    scratch += scatter_scratch(AXES, ALL_ORDERS[0], 16, 128)
    for i in range(6):
        scratch += scatter_scratch(
            rest_of(FFN_DIMS, FIRST_STAGE[i % 2][0]), LAST_STAGE[i % 2], ROWS, 768
        )
    ffn = jax.ShapeDtypeStruct((ROWS, D), F32)
    return pl.pallas_call(
        weight_grads_kernel,
        out_shape=(
            jax.ShapeDtypeStruct((16, D), F32),
            jax.ShapeDtypeStruct((16, 128), F32),
            ffn,
            ffn,
            ffn,
        ),
        in_specs=[ANY] * 8,
        out_specs=(VMEM,) * 5,
        scratch_shapes=[
            pltpu.SemaphoreType.DMA((copies,)),
            pltpu.SemaphoreType.DMA((copies,)),
            pltpu.SemaphoreType.DMA((10,)),
        ]
        + scratch,
        compiler_params=pltpu.CompilerParams(
            collective_id=6, has_side_effects=True, vmem_limit_bytes=60 * 2**20
        ),
    )(qkv, small, *parts)


def positions_of(documents):
    index = jnp.arange(documents.shape[0], dtype=jnp.int32)
    kinds = jnp.arange(doc_kinds, dtype=jnp.int32)
    counts = jnp.sum((documents[None, :] == kinds[:, None]).astype(jnp.int32), axis=1)
    starts = jnp.cumsum(counts) - counts
    first = jnp.sum(jnp.where(documents[:, None] == kinds[None, :], starts[None, :], 0), axis=1)
    return index - first


def rope_tables(position):
    half = HD // 2
    inverse = rope_base ** (-(jnp.arange(half, dtype=jnp.float32) * 2.0 / HD))
    angle = position.astype(jnp.float32)[:, None] * inverse[None, :]
    angle = jnp.concatenate([angle, angle], axis=1)
    return (jnp.cos(angle), jnp.sin(angle))


def dot(a, b, dims):
    return lax.dot_general(a, b, ((dims[:1], dims[1:]), ((), ())), preferred_element_type=F32)


def local(
    tokens_in,
    qkv_weight,
    qkv_bias,
    out_weight,
    norm_gains,
    gate_weight,
    up_weight,
    down_weight,
    doc_ids,
    cotangent,
):
    block_index = lax.axis_index("y") * 8 + lax.axis_index("x") * 2 + lax.axis_index("zh")
    inputs = tokens_in[0].astype(F32)
    documents = doc_ids[0]
    cot_low = cotangent[0]

    small = jnp.concatenate([qkv_bias, norm_gains.reshape(-1)])[None]
    small = jnp.pad(small, ((0, 15), (0, 256 - small.shape[1])))
    units, out_rows = gate_weight.shape[0], out_weight.shape[0]
    qkv_all, out_all, small_all = gather_weights(
        qkv_weight, jnp.pad(out_weight, ((0, 16 - out_rows), (0, 0))), small
    )
    w_qkv = qkv_all.reshape(2048, D)
    w_out = out_all.reshape(2048, D)
    small_all = small_all.reshape(128, 16, 256)[:, 0]
    b_qkv = small_all[:, :16].reshape(2048).astype(F32)
    gain_one = small_all[:, 16:28].reshape(D).astype(F32)
    gain_two = small_all[:, 28:40].reshape(D).astype(F32)
    feature = lax.broadcasted_iota(jnp.int32, (384, 512), 0)
    slot = lax.broadcasted_iota(jnp.int32, (384, 512), 1)
    spread = (slot == feature // out_rows * 16 + feature % out_rows).astype(BF)

    first_row = block_index * TOK
    my_pos = lax.dynamic_slice_in_dim(positions_of(documents), first_row, TOK, 0)
    cosine, sine = rope_tables(my_pos)
    sine = jnp.concatenate([-sine[:, : HD // 2], sine[:, HD // 2 :]], axis=1)
    first = first_row + jnp.arange(TOK, dtype=jnp.int32) - my_pos
    first = jnp.broadcast_to(jnp.tile(first, GROUP)[None], (8, GQ))

    factor_one = lax.rsqrt(jnp.mean(inputs * inputs, axis=-1, keepdims=True) + norm_eps)
    normed_one = (inputs * factor_one * gain_one).astype(BF)
    qkv = dot(normed_one, w_qkv, (1, 1)) + b_qkv
    pad = ((0, ROWS - units), (0, 0))
    kv, queries, attended, slots, lse, middle, w_gate, w_up, w_down, cot_rows, rows_two = attend(
        qkv,
        cosine,
        sine,
        first,
        spread,
        tokens_in[0],
        jnp.broadcast_to(gain_two[None], (8, D)),
        jnp.pad(gate_weight, pad),
        jnp.pad(up_weight, pad),
        jnp.pad(down_weight, pad),
        cot_low,
        w_out,
    )
    w_gate, w_up, w_down = (w.reshape(-1, D) for w in (w_gate, w_up, w_down))
    cot_rows, rows_two = cot_rows.reshape(-1, D), rows_two.reshape(-1, D)
    factor_two = lax.rsqrt(jnp.mean(middle * middle, axis=-1, keepdims=True) + norm_eps)

    gate = dot(rows_two, w_gate, (1, 1))
    upward = dot(rows_two, w_up, (1, 1))
    hidden_grad = dot(cot_rows, w_down, (1, 1))
    sigma = jax.nn.sigmoid(gate)
    hidden = (gate * sigma * upward).astype(BF)
    gate_grad = (hidden_grad * upward * sigma * (1.0 + gate * (1.0 - sigma))).astype(BF)
    upward_grad = (hidden_grad * gate * sigma).astype(BF)
    ffn_part = dot(hidden, w_down, (1, 0)).astype(BF)
    grad_part = (dot(gate_grad, w_gate, (1, 0)) + dot(upward_grad, w_up, (1, 0))).astype(BF)
    ffn_lead = lead_of(FFN_DIMS) + (ROWS, D)
    gate_part, up_part, down_part = (
        dot(a, b, (0, 0)).astype(BF).reshape(ffn_lead)
        for a, b in ((gate_grad, rows_two), (upward_grad, rows_two), (hidden, cot_rows))
    )
    rows_lead = lead_of(ROW_DIMS) + (TOK, D)
    normed_two_grad, *down_sums = scatter_rows(grad_part.reshape(rows_lead), down_part)

    cot_full = cot_low.astype(F32)
    scaled_two = gain_two * normed_two_grad
    gain_two_grad = jnp.sum(normed_two_grad * middle * factor_two, axis=0)
    middle_grad = (
        cot_full
        + factor_two * scaled_two
        - middle * factor_two**3 * jnp.mean(scaled_two * middle, axis=-1, keepdims=True)
    )
    branch_grad = middle_grad.astype(BF)
    grad_slots = dot(branch_grad, w_out, (1, 1)).astype(BF)
    out_part = dot(slots, branch_grad, (0, 0)).astype(BF)
    lead = lead_of(AXES)
    qkv_grad, *parts, out_sum, ffn_total = attend_back(
        kv,
        queries,
        attended,
        grad_slots,
        lse,
        first,
        cosine,
        sine,
        spread,
        gate_part,
        up_part,
        out_part.reshape(lead + (16, D)),
        ffn_part.reshape(rows_lead),
    )
    layer_out = (middle + ffn_total).astype(BF)
    normed_one_grad = dot(qkv_grad, w_qkv, (1, 0))
    scaled_one = gain_one * normed_one_grad
    gain_one_grad = jnp.sum(normed_one_grad * inputs * factor_one, axis=0)
    input_grad = (
        middle_grad
        + factor_one * scaled_one
        - inputs * factor_one**3 * jnp.mean(scaled_one * inputs, axis=-1, keepdims=True)
    )

    qkv_part = dot(qkv_grad, normed_one, (0, 0)).astype(BF)
    bias_part = jnp.sum(qkv_grad.astype(F32), axis=0)
    small_part = jnp.concatenate(
        [
            bias_part.reshape(128, 16),
            gain_one_grad.reshape(128, 12),
            gain_two_grad.reshape(128, 12),
        ],
        axis=1,
    ).astype(BF)
    small_part = jnp.pad(small_part[:, None], ((0, 0), (0, 15), (0, 88)))
    qkv_sum, small_sum, gate_sum, up_sum, down_sum = scatter_weight_grads(
        qkv_part.reshape(lead + (16, D)),
        small_part.reshape(lead + (16, 128)),
        (*parts, *down_sums),
    )
    return (
        layer_out[None],
        input_grad[None],
        qkv_sum,
        small_sum[0, :16],
        out_sum[:out_rows],
        small_sum[0, 16:40].reshape(2, 12),
        gate_sum[:units],
        up_sum[:units],
        down_sum[:units],
    )


def solution(mesh):
    fine = Mesh(mesh.devices.reshape(tuple(SIZE[a] for a in AXES)), AXES)
    dp, ctx = ("zl", "c"), ("y", "x", "zh")
    in_specs = (
        P(dp, ctx, None),
        P(AXES, None),
        P(AXES),
        P(AXES, None),
        P(None, AXES),
        P(AXES, None),
        P(AXES, None),
        P(AXES, None),
        P(dp, None),
        P(dp, ctx, None),
    )
    out_specs = (
        P(dp, ctx, None),
        P(dp, ctx, None),
        P(AXES, None),
        P(AXES),
        P(AXES, None),
        P(None, AXES),
        P(AXES, None),
        P(AXES, None),
        P(AXES, None),
    )
    return jax.shard_map(local, mesh=fine, in_specs=in_specs, out_specs=out_specs, check_vma=False)
```

time: 537 us -> 457 us (0.85)
  Pallas kernels: 416 us -> 340 us
    pallas_call x3 -> x2, Pallas kernels: 136 us -> 74.9 us  [the longest x1 43.7 us: scatter_weight_grads(): pl.pallas_call(weight_grads_kernel, out_shape=(jax.ShapeDtypeStruct((16,...]
    pallas_call x1, Pallas kernels: 112 us -> 100 us  [attend_back(): pl.pallas_call(attend_back_kernel, out_shape=(jax.ShapeDtypeStruct((TOK,...]
    pallas_call x1, Pallas kernels: 117 us -> 109 us  [attend(): pl.pallas_call(attend_kernel, out_shape=(jax.ShapeDtypeStruct(lead_of(KV_...]
    dot_general x15 -> x14, matrix products: 83 us -> 83.2 us  [dot(): lax.dot_general(a, b, ((dims[:1], dims[1:]), ((), ())), preferred_element...]
where the time goes in v3:
time: 457 us; the launch traced here: 449 us
  Pallas kernels  340 us (74%)
  matrix products  83.2 us (18%)
  local copies, waits for them, and re-layouts  15.3 us (3%)
  other arithmetic  9.04 us (2%)
    pallas_call x1, Pallas kernels, attend(): pl.pallas_call(attend_kernel, out_shape=(jax.ShapeDtypeStruct(lead_of(KV_...  109 us
    pallas_call x1, Pallas kernels, attend_back(): pl.pallas_call(attend_back_kernel, out_shape=(jax.ShapeDtypeStruct((TOK,...  100 us
    dot_general x14, matrix products, dot(): lax.dot_general(a, b, ((dims[:1], dims[1:]), ((), ())), preferred_element...  83.2 us
    pallas_call x1, Pallas kernels, gather_weights(): pl.pallas_call(weights_kernel, out_shape=(every, every, smalls), in_specs...  55.2 us
    pallas_call x1, Pallas kernels, scatter_weight_grads(): pl.pallas_call(weight_grads_kernel, out_shape=(jax.ShapeDtypeStruct((16,...  43.7 us
    pallas_call x1, Pallas kernels, scatter_rows(): pl.pallas_call(rows_scatter_kernel, out_shape=(jax.ShapeDtypeStruct((TOK,...  31.2 us

profile of v3, /device:TPU:0, one launch (start us, length us, event | category | flops | bytes accessed | tf_op | source)
XLA Modules:
  0.0 448.8 jit_solution(4520554136856347883)
XLA Ops:
  0.6 0.9 convert_reduce_fusion
  1.5 0.2 reduce-window.8
  1.7 0.8 select_reduce_fusion
  2.5 0.1 add_subtract_fusion
  2.6 0.1 broadcast_multiply_fusion
  2.7 0.3 fusion.20
  3.0 0.0 copy-start.4
  3.1 0.1 slice_negate_fusion
  3.1 0.1 pad_maximum_fusion.1.refs_2_.refs_7_
  3.3 0.0 copy-start.9
  3.3 1.4 pad.22.out
  4.7 0.7 reshape.233
  5.4 0.7 maximum_bitcast_fusion
  6.2 0.6 pad.23.small
  6.8 55.2 %shard_map.169 = (bf16[2,2,4,4,2,16,1536]{6,5,4,3,2,1,0:T(8,128)(2,1)}, bf16[2,2,4,4,2,16,1536]{6,5,4,3,2,1,0:T(8,128)(2,1)}, bf16[2,2,4,4,2,16,256]{6,5,4,3,2,1,0:T(8,128)(2,1)}) custom-call(bf16[16,1536]{1,0:T(8,128)(2,1)} %qkv.1, bf16[16,1536]{1,0:T(8,128)(2,1)} %pad.22.out, bf16[16,256]{1,0:T(8,128)(2,1)} %pad.23.small), custom_call_target="tpu_custom_call" | custom-call | tf_op jit(solution)/shard_map/pallas_call | solution.py:172
  62.0 1.1 slice.48
  63.1 0.1 slice_convert_fusion
  63.2 0.1 reshape.252
  63.3 1.2 fusion
  64.5 0.1 reshape.253
  64.6 0.0 copy-start.14
  64.6 0.0 copy-start
  64.6 5.2 %convolution_add_fusion.refs_0_ = f32[128,2048]{1,0:T(8,128)S(1)} fusion(bf16[2048,1536]{1,0:T(8,128)(2,1)} %bitcast.77, f32[2048]{0:T(1024)S(1)} %reshape.253, bf16[1,128,1536]{2,1,0:T(8,128)(2,1)} %param.10, f32[1536]{0:T(1024)S(1)} %reshape.252, f32[128]{0:T(128)S(1)} %get-tuple-element.83), kind=kOutput, calls=%fused_computation.11 | convolution fusion | flops 806354944 | bytes 7748096 | tf_op jit(solution)/shard_map/dot_general | solution.py:742
  69.9 0.5 fusion.9.refs_4_.refs_8_
  70.4 0.1 reshape.254
  70.7 109.5 %shard_map.170 = (bf16[4,4,2,128,512]{4,3,2,1,0:T(8,128)(2,1)}, bf16[128,1536]{1,0:T(8,128)(2,1)S(1)}, f32[128,1536]{1,0:T(8,128)S(1)}, bf16[128,2048]{1,0:T(8,1...) custom-call(f32[128,2048]{1,0:T(8,128)S(1)} %convolution_add_fusion., ...), custom_call_target="tpu_custom_call" | custom-call | tf_op jit(solution)/shard_map/pallas_call | solution.py:475
  180.2 10.1 %fusion.30 = f32[1024,1280]{1,0:T(8,128)} fusion(bf16[1024,1536]{1,0:T(8,128)(2,1)} %bitcast.105, bf16[1280,1536]{1,0:T(8,128)(2,1)} %bitcast.99), kind=kOutput, calls=%fused_computation.84 | convolution fusion | flops 4026531840 | bytes 12320768 | tf_op jit(solution)/shard_map/dot_general | solution.py:742
  190.4 6.2 %fusion.31 = f32[1024,1280]{1,0:T(8,128)} fusion(bf16[1024,1536]{1,0:T(8,128)(2,1)S(1)} %bitcast.101, bf16[1280,1536]{1,0:T(8,128)(2,1)S(1)} %bitcast.97), kind=kOutput, calls=%fused_computation.85 | convolution fusion | flops 4026531840 | bytes 12320768 | tf_op jit(solution)/shard_map/dot_general | solution.py:742
  196.6 10.7 %multiply_convert_fusion = (bf16[1024,1280]{1,0:T(8,128)(2,1)}, bf16[1024,1280]{1,0:T(8,128)(2,1)}, bf16[1024,1280]{1,0:T(8,128)(2,1)}) fusion(f32[1024,1280]{1,0:T(8,128)} %fusion.31, f32[1024,1280]{1,0:T(8,128)} %fusion.30, bf16[1024,1536]{1,0:T(8,128)(2,1)S(1)} %bitcast.102, bf16[1280,1536]{1,0:T(8,128)(2,1)S(1)} %bitcast.95), kind=kOutput, calls=%fused_computation.6 | convolution fusion | flops 4047503360 | bytes 25427968 | tf_op jit(solution)/shard_map/dot_general | solution.py:742
  207.4 7.6 %convolution_convert_fusion.5 = bf16[1024,1536]{1,0:T(8,128)(2,1)} fusion(bf16[1024,1280]{1,0:T(8,128)(2,1)} %get-tuple-element.71, bf16[1280,1536]{1,0:T(8,128)(2,1)S(1)} %bitcast.100), kind=kOutput, calls=%fused_computation.10 | convolution fusion | flops 4028104704 | bytes 9699328 | tf_op jit(solution)/shard_map/dot_general | solution.py:742
  214.9 5.9 %convolution_convert_fusion.2 = bf16[1280,1536]{1,0:T(8,128)(2,1)} fusion(bf16[1024,1280]{1,0:T(8,128)(2,1)S(1)} %copy-done.26, bf16[1024,1536]{1,0:T(8,128)(2,1)S(1)} %bitcast.106), kind=kOutput, calls=%fused_computation.2 | convolution fusion | flops 4028497920 | bytes 9699328 | tf_op jit(solution)/shard_map/dot_general | solution.py:742
  220.9 4.2 fusion.32
  225.1 4.5 add_convert_fusion
  229.6 31.2 %shard_map.171 = (f32[128,1536]{1,0:T(8,128)S(1)}, bf16[2,2,80,768]{3,2,1,0:T(8,128)(2,1)S(1)}, bf16[4,80,768]{2,1,0:T(8,128)(2,1)S(1)}) custom-call(bf16[4,2,128,1536]{3,2,1,0:T(8,128)(2,1)S(1)} %bitcast.73, bf16[2,4,2,80,1536]{4,3,2,1,0:T(8,128)(2,1)} %bitcast.83), custom_call_target="tpu_custom_call" | custom-call | tf_op jit(solution)/shard_map/pallas_call | solution.py:305
  260.8 0.1 multiply_reduce_fusion.2
  261.0 0.2 multiply_reduce_fusion
  261.2 0.3 multiply_subtract_fusion
  261.5 4.5 convolution_convert_fusion.4
  266.0 5.9 %convolution_convert_fusion = bf16[1280,1536]{1,0:T(8,128)(2,1)} fusion(bf16[1024,1280]{1,0:T(8,128)(2,1)S(1)} %copy-done.23, bf16[1024,1536]{1,0:T(8,128)(2,1)S(1)} %bitcast.103), kind=kOutput, calls=%fused_computation | convolution fusion | flops 4028497920 | bytes 9699328 | tf_op jit(solution)/shard_map/dot_general | solution.py:742
  271.9 6.0 %convolution_convert_fusion.1 = bf16[1280,1536]{1,0:T(8,128)(2,1)} fusion(bf16[1024,1280]{1,0:T(8,128)(2,1)S(1)} %copy-done.25, bf16[1024,1536]{1,0:T(8,128)(2,1)S(1)} %bitcast.104), kind=kOutput, calls=%fused_computation.1 | convolution fusion | flops 4028497920 | bytes 9699328 | tf_op jit(solution)/shard_map/dot_general | solution.py:742
  277.9 3.0 convolution_convert_fusion.6.refs_3_
  280.9 100.1 %shard_map.172 = (bf16[128,2048]{1,0:T(8,128)(2,1)}, bf16[2,2,80,768]{3,2,1,0:T(8,128)(2,1)}, bf16[4,80,768]{2,1,0:T(8,128)(2,1)}, bf16[2,2,80,768]{3,2,1,0:T(8,...) custom-call(bf16[4,4,2,128,512]{4,3,2,1,0:T(8,128)(2,1)} %get-tuple-element.42.refs_0_, ...), custom_call_target="tpu_custom_call" | custom-call | tf_op jit(solution)/shard_map/pallas_call | solution.py:630
  381.0 4.9 %fusion.8 = (bf16[1536]{0:T(1024)(128)(2,1)S(1)}, f32[128]{0:T(128)S(1)}, f32[128,1536]{1,0:T(8,128)}) fusion(f32[128]{0:T(128)S(1)} %get-tuple-element.83, bf16[1,128,1536]{2,1,0:T(8,128)(2,1)S(1)} %copy-done, f32[1536]{0:T(1024)S(1)} %reshape.252, bf16[128,2048]{1,0:T(8,128)(2,1)} %get-tuple-element.54, bf16[2048,1536]{1,0:T(8,128)(2,1)} %bitcast.78), kind=kOutput, calls=%fused_computation.26 | convolution fusion | flops 806680960 | bytes 8005632 | tf_op jit(solution)/shard_map/dot_general | solution.py:742
  385.9 0.1 concatenate.30
  386.0 0.1 copy.28
  386.1 0.1 reduce
  386.2 0.1 concatenate.29
  386.3 0.1 copy.27
  386.4 0.1 concatenate.31
  386.5 0.1 copy.29
  386.6 0.1 copy.32
  386.8 0.9 pad.27.clone
  387.6 4.6 %convolution_convert_fusion.3 = bf16[2048,1536]{1,0:T(8,128)(2,1)} fusion(bf16[128,2048]{1,0:T(8,128)(2,1)S(1)} %copy-done.11, f32[1536]{0:T(1024)S(1)} %reshape.252, f32[128]{0:T(128)S(1)} %get-tuple-element.83, bf16[1,128,1536]{2,1,0:T(8,128)(2,1)S(1)} %copy-done), kind=kOutput, calls=%fused_computation.3 | convolution fusion | flops 809238528 | bytes 7215616 | tf_op jit(solution)/shard_map/dot_general | solution.py:742
  392.2 43.7 %shard_map.173 = (f32[16,1536]{1,0:T(8,128)}, f32[16,128]{1,0:T(8,128)}, f32[80,1536]{1,0:T(8,128)}, f32[80,1536]{1,0:T(8,128)}, f32[80,1536]{1,0:T(8,128)}) custom-call(bf16[2,2,4,4,2,16,1536]{6,5,4,3,2,1,0:T(8,128)(2,1)} %bitcast.75, bf16[2,2,4,4,2,16,128]{6,5,4,3,2,1,0:T(8,128)(2,1)} %bitcast.87, bf16[2,2,80,768]{3,2,1,0:T(8,128)(2,1)} %get-tuple-element.55.refs_2_, ...), custom_call_target="tpu_custom_call" | custom-call | tf_op jit(solution)/shard_map/pallas_call | solution.py:701
  435.9 1.8 slice.45
  437.8 1.8 slice.46
  439.6 1.8 slice.47
  441.4 0.8 slice_reduce_fusion
  442.2 0.6 reshape_squeeze.3
  442.8 1.2 slice_bitcast_fusion
  444.0 1.1 fusion.3
  445.1 2.0 fusion.12
  447.1 0.6 copy.37
  447.7 0.6 copy.38
  (73 shorter events, 0.3 us)
Async XLA Ops:
  3.0 67.6 %copy-start.4 = (f32[128,128]{1,0:T(8,128)}, f32[128,128]{1,0:T(8,128)S(1)}, u32[]{:S(2)}) copy-start(f32[128,128]{1,0:T(8,128)S(1)} %get-tuple-element.79.refs_1_.refs_6_) | copy-start | bytes 196612
  3.2 67.4 %copy-start.5 = (f32[128,128]{1,0:T(8,128)}, f32[128,128]{1,0:T(8,128)S(1)}, u32[]{:S(2)}) copy-start(f32[128,128]{1,0:T(8,128)S(1)} %pad_maximum_fusion.1.refs_2_.refs_7_) | copy-start | bytes 196612
  3.3 67.4 %copy-start.9 = (s32[8,768]{1,0:T(8,128)}, s32[8,768]{1,0:T(8,128)S(1)}, u32[]{:S(2)}) copy-start(s32[8,768]{1,0:T(8,128)S(1)} %broadcast_in_dim.28.refs_3_.refs_5_) | copy-start | bytes 73732
  64.6 6.0 %copy-start.13 = (bf16[70,1536]{1,0:T(8,128)(2,1)S(1)}, bf16[70,1536]{1,0:T(8,128)(2,1)}, u32[]{:S(2)}) copy-start(bf16[70,1536]{1,0:T(8,128)(2,1)} %param.15) | copy-start | bytes 645124
  64.6 6.0 %copy-start.14 = (bf16[70,1536]{1,0:T(8,128)(2,1)S(1)}, bf16[70,1536]{1,0:T(8,128)(2,1)}, u32[]{:S(2)}) copy-start(bf16[70,1536]{1,0:T(8,128)(2,1)} %param.16) | copy-start | bytes 645124
  64.6 6.0 %copy-start.15 = (bf16[70,1536]{1,0:T(8,128)(2,1)S(1)}, bf16[70,1536]{1,0:T(8,128)(2,1)}, u32[]{:S(2)}) copy-start(bf16[70,1536]{1,0:T(8,128)(2,1)} %param.17) | copy-start | bytes 645124
  64.6 6.1 %copy-start = (bf16[1,128,1536]{2,1,0:T(8,128)(2,1)S(1)}, bf16[1,128,1536]{2,1,0:T(8,128)(2,1)}, u32[]{:S(2)}) copy-start(bf16[1,128,1536]{2,1,0:T(8,128)(2,1)} %param.10) | copy-start | bytes 1179652
  64.6 6.1 %copy-start.2 = (bf16[1,128,1536]{2,1,0:T(8,128)(2,1)S(1)}, bf16[1,128,1536]{2,1,0:T(8,128)(2,1)}, u32[]{:S(2)}) copy-start(bf16[1,128,1536]{2,1,0:T(8,128)(2,1)} %param.19) | copy-start | bytes 1179652
  70.4 109.8 %copy-start.1 = (bf16[384,512]{1,0:T(8,128)(2,1)}, bf16[384,512]{1,0:T(8,128)(2,1)S(1)}, u32[]{:S(2)}) copy-start(bf16[384,512]{1,0:T(8,128)(2,1)S(1)} %fusion.9.refs_4_.refs_8_) | copy-start | bytes 1179652
  180.2 10.2 %copy-start.3 = (f32[128,1536]{1,0:T(8,128)}, f32[128,1536]{1,0:T(8,128)S(1)}, u32[]{:S(2)}) copy-start(f32[128,1536]{1,0:T(8,128)S(1)} %get-tuple-element.44.refs_2_) | copy-start | bytes 2359300
  180.2 10.2 %copy-start.8 = (bf16[128,1536]{1,0:T(8,128)(2,1)}, bf16[128,1536]{1,0:T(8,128)(2,1)S(1)}, u32[]{:S(2)}) copy-start(bf16[128,1536]{1,0:T(8,128)(2,1)S(1)} %get-tuple-element.43.refs_1_) | copy-start | bytes 1179652
  180.2 10.2 %copy-start.10 = (f32[2,8,768]{2,1,0:T(8,128)}, f32[2,8,768]{2,1,0:T(8,128)S(1)}, u32[]{:S(2)}) copy-start(f32[2,8,768]{2,1,0:T(8,128)S(1)} %get-tuple-element.51.refs_4_) | copy-start | bytes 147460
  180.2 10.2 %copy-start.19 = (bf16[2,4,2,80,1536]{4,3,2,1,0:T(8,128)(2,1)S(1)}, bf16[2,4,2,80,1536]{4,3,2,1,0:T(8,128)(2,1)}, u32[]{:S(2)}) copy-start(bf16[2,4,2,80,1536]{4,3,2,1,0:T(8,128)(2,1)} %get-tuple-element.49) | copy-start | bytes 11796484
  180.2 10.2 %copy-start.21 = (bf16[4,2,128,1536]{3,2,1,0:T(8,128)(2,1)S(1)}, bf16[4,2,128,1536]{3,2,1,0:T(8,128)(2,1)}, u32[]{:S(2)}) copy-start(bf16[4,2,128,1536]{3,2,1,0:T(8,128)(2,1)} %get-tuple-element.47) | copy-start | bytes 9437188
  190.4 6.2 %copy-start.18 = (bf16[2,4,2,80,1536]{4,3,2,1,0:T(8,128)(2,1)S(1)}, bf16[2,4,2,80,1536]{4,3,2,1,0:T(8,128)(2,1)}, u32[]{:S(2)}) copy-start(bf16[2,4,2,80,1536]{4,3,2,1,0:T(8,128)(2,1)} %get-tuple-element.48) | copy-start | bytes 11796484
  196.6 10.8 %copy-start.20 = (bf16[2,4,2,80,1536]{4,3,2,1,0:T(8,128)(2,1)S(1)}, bf16[2,4,2,80,1536]{4,3,2,1,0:T(8,128)(2,1)}, u32[]{:S(2)}) copy-start(bf16[2,4,2,80,1536]{4,3,2,1,0:T(8,128)(2,1)} %get-tuple-element.46) | copy-start | bytes 11796484
  207.3 7.6 %copy-start.22 = (bf16[4,2,128,1536]{3,2,1,0:T(8,128)(2,1)S(1)}, bf16[4,2,128,1536]{3,2,1,0:T(8,128)(2,1)}, u32[]{:S(2)}) copy-start(bf16[4,2,128,1536]{3,2,1,0:T(8,128)(2,1)} %get-tuple-element.45) | copy-start | bytes 9437188
  207.3 7.6 %copy-start.26 = (bf16[1024,1280]{1,0:T(8,128)(2,1)S(1)}, bf16[1024,1280]{1,0:T(8,128)(2,1)}, u32[]{:S(2)}) copy-start(bf16[1024,1280]{1,0:T(8,128)(2,1)} %get-tuple-element.71) | copy-start | bytes 7864324
  214.9 5.9 %copy-start.24 = (bf16[1024,1280]{1,0:T(8,128)(2,1)S(1)}, bf16[1024,1280]{1,0:T(8,128)(2,1)}, u32[]{:S(2)}) copy-start(bf16[1024,1280]{1,0:T(8,128)(2,1)} %get-tuple-element.72) | copy-start | bytes 7864324
  220.9 4.2 copy-start.23
  260.8 5.2 %copy-start.6 = (bf16[2,2,80,768]{3,2,1,0:T(8,128)(2,1)}, bf16[2,2,80,768]{3,2,1,0:T(8,128)(2,1)S(1)}, u32[]{:S(2)}) copy-start(bf16[2,2,80,768]{3,2,1,0:T(8,128)(2,1)S(1)} %get-tuple-element.59.refs_6_) | copy-start | bytes 1474564
  260.8 5.2 %copy-start.7 = (bf16[4,80,768]{2,1,0:T(8,128)(2,1)}, bf16[4,80,768]{2,1,0:T(8,128)(2,1)S(1)}, u32[]{:S(2)}) copy-start(bf16[4,80,768]{2,1,0:T(8,128)(2,1)S(1)} %get-tuple-element.60.refs_7_) | copy-start | bytes 1474564
  266.0 5.9 %copy-start.25 = (bf16[1024,1280]{1,0:T(8,128)(2,1)S(1)}, bf16[1024,1280]{1,0:T(8,128)(2,1)}, u32[]{:S(2)}) copy-start(bf16[1024,1280]{1,0:T(8,128)(2,1)} %get-tuple-element.72) | copy-start | bytes 7864324
  266.0 11.9 %slice-start = ((s8[6291456]{0:T(1024)(128)(4,1)}), s8[4194304]{0:T(1024)(128)(4,1)S(1)}, s32[]{:S(2)}) async-start(s8[6291456]{0:T(1024)(128)(4,1)} %bitcast.80), calls=%async_computation | async-start | bytes 8388608
  271.9 6.0 %slice-start.1 = ((s8[6291456]{0:T(1024)(128)(4,1)}), s8[2097152]{0:T(1024)(128)(4,1)S(1)}, s32[]{:S(2)}) async-start(s8[6291456]{0:T(1024)(128)(4,1)} %bitcast.80), calls=%async_computation.1 | async-start | bytes 4194304
  381.0 5.1 %copy-start.11 = (bf16[128,2048]{1,0:T(8,128)(2,1)S(1)}, bf16[128,2048]{1,0:T(8,128)(2,1)}, u32[]{:S(2)}) copy-start(bf16[128,2048]{1,0:T(8,128)(2,1)} %get-tuple-element.54) | copy-start | bytes 1572868
  392.2 51.8 %copy-start.12 = (f32[128,1536]{1,0:T(8,128)S(1)}, f32[128,1536]{1,0:T(8,128)}, u32[]{:S(2)}) copy-start(f32[128,1536]{1,0:T(8,128)} %get-tuple-element.86) | copy-start | bytes 2359300
  435.9 11.2 %copy-start.17 = (f32[16,1536]{1,0:T(8,128)S(1)}, f32[16,1536]{1,0:T(8,128)}, u32[]{:S(2)}) copy-start(f32[16,1536]{1,0:T(8,128)} %get-tuple-element.104) | copy-start | bytes 294916
  435.9 11.8 %copy-start.16 = (f32[16,1536]{1,0:T(8,128)S(1)}, f32[16,1536]{1,0:T(8,128)}, u32[]{:S(2)}) copy-start(f32[16,1536]{1,0:T(8,128)} %get-tuple-element.63) | copy-start | bytes 294916
